TPU v7x, 256 devices: a whole 4x4x8 slice. The times are simulated.
256 devices in a mesh: gz: 64 (over x, z, core), gy: 4 (over y).
Axes of the slice: x: 4, y: 4, z: 8, core: 2. Of those that a mesh axis runs over, the one named last changes fastest.
Arguments:
- charges: float32 [65536], P(('gz', 'gy')), may hold values from -6 to 6
- grid_base: int32 [3, 65536], P(None, ('gz', 'gy')), may hold values from 0 to 511, as said below
- fraction: float32 [3, 65536], P(None, ('gz', 'gy')), may hold values from 0 to 1
- counts: int32 [64, 4], P('gz', 'gy'), may hold values from 128 to 256, as said below
- influence: float32 [512, 256, 512], P(None, ('gy', 'gz')), may hold values from 200 to 2000
Outputs:
- forces: float32 [3, 65536], P(None, ('gz', 'gy'))
Inputs may be any that keep to these rules, and one draw needn't show every extreme that they name: `grid_base`: rows are z, y, x. The slots of block d = s // 256, with d = g * 4 + h, have z base in [g * 8, (g + 1) * 8) and y base in [h * 128, (h + 1) * 128); x base is any cell, padding slots included. `counts`: live slots of each block; slots at or past the count are padding. Some block is full in every draw.
All inputs are finite; a program needn't handle non-finite values.
Results may differ from a plain program's by a relative error of at most 0.0003.
Values sent between devices are 32-bit elements; how exact they have to be, the bound alone decides.
A program may use at most 128 MiB of HBM per device.

v0:
```python
import math

import jax
import jax.numpy as jnp
from jax import lax
from jax.sharding import PartitionSpec as P

KX = 512
KY = 512
KZ = 512
ORDER = 6
MARGIN = 5
XH = 256


def from_behind(block, axis, distance):
    devices = range(lax.axis_size(axis))
    route = [((i - distance) % len(devices), i) for i in devices]
    return lax.ppermute(block, axis, route)


def spline_six(offset):
    values = [jnp.ones_like(offset)]
    slopes = values
    for k in range(2, ORDER + 1):
        previous = values
        if k == ORDER:
            slopes = [
                (previous[j - 1] if j > 0 else 0.0) - (previous[j] if j < k - 1 else 0.0)
                for j in range(k)
            ]
        values = []
        for j in range(k):
            lower_term = previous[j - 1] if j > 0 else 0.0
            upper_term = previous[j] if j < k - 1 else 0.0
            values.append(
                ((offset + (k - 1 - j)) * lower_term + (1.0 + j - offset) * upper_term) / (k - 1)
            )
    return (jnp.stack(values), jnp.stack(slopes))


def weight_table(index, weights, length):
    cells = jnp.arange(length, dtype=jnp.int32)
    hits = (index[:, None, :] == cells[None, :, None]).astype(jnp.float32)
    return jnp.sum(hits * weights[:, None, :], axis=0)


def phase_table(positions, freqs, length, scale):
    turns = positions[:, None] * freqs[None, :] % length
    angle = turns.astype(jnp.float32) * (2.0 * math.pi / length)
    return (scale * jnp.cos(angle), scale * jnp.sin(angle))


def einsum_high(form, left_arr, right_arr):
    return jnp.einsum(form, left_arr, right_arr, precision=lax.Precision.HIGHEST)


def forward_pair(stacked, table, form):
    cos_tab, sin_tab = table
    real_out = einsum_high(form, stacked[0], cos_tab) + einsum_high(form, stacked[1], sin_tab)
    imag_out = einsum_high(form, stacked[1], cos_tab) - einsum_high(form, stacked[0], sin_tab)
    return jnp.stack([real_out, imag_out])


def inverse_pair(stacked, table, form):
    cos_tab, sin_tab = table
    real_out = einsum_high(form, stacked[0], cos_tab) - einsum_high(form, stacked[1], sin_tab)
    imag_out = einsum_high(form, stacked[1], cos_tab) + einsum_high(form, stacked[0], sin_tab)
    return jnp.stack([real_out, imag_out])


def fold_axis(stacked, axis, blocks, inner):
    shape = stacked.shape
    parts = stacked.reshape(shape[:axis] + (blocks, inner + MARGIN) + shape[axis + 1 :])
    main = lax.slice_in_dim(parts, 0, inner, axis=axis + 1)
    extra = jnp.roll(lax.slice_in_dim(parts, inner, inner + MARGIN, axis=axis + 1), 1, axis=axis)
    head = lax.slice_in_dim(main, 0, MARGIN, axis=axis + 1) + extra
    tail = lax.slice_in_dim(main, MARGIN, inner, axis=axis + 1)
    joined = jnp.concatenate([head, tail], axis=axis + 1)
    return joined.reshape(shape[:axis] + (blocks * inner,) + shape[axis + 1 :])


def extended_positions(blocks, inner, length):
    index = jnp.arange(blocks * (inner + MARGIN), dtype=jnp.int32)
    return (index // (inner + MARGIN) * inner + index % (inner + MARGIN)) % length


def local(charges, grid_base, fraction, counts, influence):
    slabs = lax.axis_size("gz")
    pencils = lax.axis_size("gy")
    slab_index = lax.axis_index("gz")
    pencil_index = lax.axis_index("gy")
    planes = KZ // slabs
    rows = KY // pencils
    row_count = rows + MARGIN
    plane_count = planes + MARGIN
    atom_slots = charges.shape[0]
    slots = jnp.arange(atom_slots, dtype=jnp.int32)
    charge = jnp.where(slots < counts[0, 0], charges, jnp.zeros_like(charges))
    steps_all = jnp.arange(ORDER, dtype=jnp.int32)
    plane_index = grid_base[0][None, :] - slab_index * planes + steps_all[:, None]
    row_index = grid_base[1][None, :] - pencil_index * rows + steps_all[:, None]
    column_index = (grid_base[2][None, :] + steps_all[:, None]) % KX
    weight_z, slope_z = spline_six(fraction[0])
    weight_y, slope_y = spline_six(fraction[1])
    weight_x, slope_x = spline_six(fraction[2])
    plane_weights = weight_table(plane_index, weight_z, plane_count)
    plane_slopes = weight_table(plane_index, slope_z, plane_count)
    row_weights = weight_table(row_index, weight_y, row_count)
    row_slopes = weight_table(row_index, slope_y, row_count)
    column_weights = weight_table(column_index, weight_x, KX)
    column_slopes = weight_table(column_index, slope_x, KX)
    charged_planes = plane_weights * charge[None, :]
    plane_rows = (charged_planes[:, None, :] * row_weights[None, :, :]).reshape(
        plane_count * row_count, atom_slots
    )
    spread = einsum_high("ca,xa->cx", plane_rows, column_weights).reshape(
        plane_count, row_count, KX
    )
    moved = from_behind(spread[planes:], "gz", 1)
    spread = jnp.concatenate([spread[:MARGIN] + moved, spread[MARGIN:planes]], axis=0)
    columns = jnp.arange(KX, dtype=jnp.int32)
    x_freqs = jnp.arange(XH, dtype=jnp.int32)
    cos_x, sin_x = phase_table(columns, x_freqs, KX, 1.0)
    spectrum = jnp.stack(
        [einsum_high("zyx,xk->zky", spread, cos_x), -einsum_high("zyx,xk->zky", spread, sin_x)]
    )
    spectrum = lax.all_to_all(spectrum, "gy", split_axis=2, concat_axis=3, tiled=True)
    spectrum = fold_axis(spectrum, 3, pencils, rows)
    y_all = jnp.arange(KY, dtype=jnp.int32)
    spectrum = forward_pair(spectrum, phase_table(y_all, y_all, KY, 1.0), "zxy,yk->zxk")
    spectrum = lax.all_to_all(spectrum, "gz", split_axis=2, concat_axis=1, tiled=True)
    z_all = jnp.arange(KZ, dtype=jnp.int32)
    spectrum = forward_pair(spectrum, phase_table(z_all, z_all, KZ, 1.0), "zxy,zk->kxy")
    spectrum = spectrum * influence[None]
    spectrum = inverse_pair(spectrum, phase_table(z_all, z_all, KZ, 1.0 / KZ), "kxy,zk->zxy")
    spectrum = lax.all_to_all(spectrum, "gz", split_axis=1, concat_axis=2, tiled=True)
    y_targets = extended_positions(pencils, rows, KY)
    spectrum = inverse_pair(spectrum, phase_table(y_targets, y_all, KY, 1.0 / KY), "zxk,yk->zxy")
    spectrum = lax.all_to_all(spectrum, "gy", split_axis=3, concat_axis=2, tiled=True)
    doubled = jnp.where(x_freqs == 0, 1.0, 2.0).astype(jnp.float32)
    cos_back, sin_back = phase_table(columns, x_freqs, KX, 1.0 / KX)
    cos_back = cos_back * doubled[None, :]
    sin_back = sin_back * doubled[None, :]
    potential = einsum_high("zky,xk->zyx", spectrum[0], cos_back) - einsum_high(
        "zky,xk->zyx", spectrum[1], sin_back
    )
    upper_rim = from_behind(potential[:MARGIN], "gz", -1)
    potential = jnp.concatenate([potential, upper_rim], axis=0)
    flat_potential = potential.reshape(plane_count * row_count, KX)
    along_weights = einsum_high("cx,xa->ca", flat_potential, column_weights).reshape(
        plane_count, row_count, atom_slots
    )
    along_slopes = einsum_high("cx,xa->ca", flat_potential, column_slopes).reshape(
        plane_count, row_count, atom_slots
    )
    rows_weighted = jnp.sum(along_weights * row_weights[None, :, :], axis=1)
    rows_sloped = jnp.sum(along_weights * row_slopes[None, :, :], axis=1)
    rows_x_sloped = jnp.sum(along_slopes * row_weights[None, :, :], axis=1)
    force_z = jnp.sum(plane_slopes * rows_weighted, axis=0)
    force_y = jnp.sum(plane_weights * rows_sloped, axis=0)
    force_x = jnp.sum(plane_weights * rows_x_sloped, axis=0)
    return -charge[None, :] * jnp.stack([force_z, force_y, force_x])


def solution(mesh):
    placed = (
        P(("gz", "gy")),
        P(None, ("gz", "gy")),
        P(None, ("gz", "gy")),
        P("gz", "gy"),
        P(None, ("gy", "gz"), None),
    )
    return jax.shard_map(
        local, mesh=mesh, in_specs=placed, out_specs=P(None, ("gz", "gy")), check_vma=False
    )
```

profile of v0, /device:TPU:1, one launch (start us, length us, event | category | flops | bytes accessed | tf_op | source)
XLA Modules:
  0.0 464.1 jit_solution(16369779199512761431)
XLA Ops:
  9.8 1.2 fusion.206
  14.0 1.5 mul.1354
  15.6 1.6 select_reduce_fusion
  17.9 4.5 fusion.211
  22.4 1.8 fusion.208
  24.2 2.6 slice.114
  26.8 3.2 collective-permute-start
  30.0 1.0 slice.134
  31.0 2.2 slice.116
  33.4 12.3 %collective-permute-done = f32[5,133,512]{2,1,0:T(8,128)} collective-permute-done((f32[5,133,512]{2,1,0:T(8,128)}, f32[5,133,512]{2,1,0:T(8,128)}, u32[]{:S(2)}, u32[]{:S(2)}) %collective-permute-start) | collective-permute-done | bytes 1361952 | tf_op jit(solution)/shard_map/ppermute | solution.py:19
  45.7 1.6 add.907
  47.4 3.8 fusion.9
  51.1 3.8 fusion.7
  55.1 3.5 copy.44
  58.6 48.0 %all_to_all.60 = f32[2,8,256,133]{3,1,0,2:T(8,128)} all-to-all(f32[2,8,256,133]{3,1,0,2:T(8,128)} %copy.44), channel_id=1, replica_groups=mesh['gz'=64,'gy'=4] {'gy'}, dimensions={2} | all-to-all | bytes 4358144 | tf_op jit(solution)/shard_map/all_to_all | solution.py:128
  106.6 8.6 %copy.57 = f32[2,8,4,64,133]{3,2,1,4,0:T(4,128)} copy(f32[2,8,4,64,133]{4,1,0,3,2:T(8,128)} %bitcast.135) | data formatting | bytes 4358144 | tf_op jit(solution)/shard_map/all_to_all | solution.py:128
  116.1 1.0 slice.136
  117.1 3.1 slice.138
  120.1 1.0 slice_add_fusion
  121.2 2.2 fusion.2
  123.4 2.1 copy.47
  125.5 1.4 squeeze.16
  126.9 7.9 %fusion.36 = f32[8,64,512]{2,1,0:T(8,128)} fusion(f32[8,64,512]{2,1,0:T(8,128)} %squeeze.16), kind=kOutput, calls=%fused_computation.80 | convolution fusion | flops 1614282752 | bytes 2097152 | tf_op jit(solution)/shard_map/zxy,yk->zxk/dot_general | solution.py:55
  134.8 1.0 copy.46
  136.3 6.3 %fusion.38 = f32[8,64,512]{2,1,0:T(8,128)S(1)} fusion(f32[8,64,512]{2,1,0:T(8,128)S(1)} %squeeze.15), kind=kOutput, calls=%fused_computation.82 | convolution fusion | flops 1614282752 | bytes 2097152 | tf_op jit(solution)/shard_map/zxy,yk->zxk/dot_general | solution.py:55
  142.7 6.7 %fusion.14 = f32[1,8,64,512]{3,2,1,0:T(8,128)S(1)} fusion(f32[8,64,512]{2,1,0:T(8,128)S(1)} %copy-done.15, f32[8,64,512]{2,1,0:T(8,128)S(1)} %squeeze.15), kind=kOutput, calls=%fused_computation.48 | convolution fusion | flops 1614544896 | bytes 3145728 | tf_op jit(solution)/shard_map/zxy,yk->zxk/dot_general | solution.py:55
  149.4 6.3 %fusion.15 = f32[1,8,64,512]{3,2,1,0:T(8,128)S(1)} fusion(f32[8,64,512]{2,1,0:T(8,128)S(1)} %fusion.38, f32[8,64,512]{2,1,0:T(8,128)S(1)} %copy-done.5), kind=kOutput, calls=%fused_computation.50 | convolution fusion | flops 1614544896 | bytes 3145728 | tf_op jit(solution)/shard_map/zxy,yk->zxk/dot_general | solution.py:55
  156.0 2.6 copy.48
  158.6 18.4 %all-to-all-start.1 = ((f32[2,8,64,512]{3,1,0,2:T(8,128)}), f32[2,8,64,512]{3,1,0,2:T(8,128)S(1)}, u32[]{:S(2)}, u32[]{:S(2)}) async-start(f32[2,8,64,512]{3,1,0,2:T(8,128)} %copy.48), calls=%async_computation.1 | async-start | bytes 4194304 | tf_op jit(solution)/shard_map/all_to_all | solution.py:132
  176.9 1.3 copy.72
  178.2 49.8 %all-to-all-done.1 = f32[2,8,64,512]{3,1,0,2:T(8,128)S(1)} async-done(((f32[2,8,64,512]{3,1,0,2:T(8,128)}), f32[2,8,64,512]{3,1,0,2:T(8,128)S(1)}, u32[]{:S(2)}, u32[]{:S(2)}) %all-to-all-start.1) | async-done | bytes 2097184 | tf_op jit(solution)/shard_map/all_to_all | solution.py:132
  228.2 5.7 %fusion.44 = f32[512,512]{1,0:T(8,128)S(1)} fusion(f32[2,64,8,1,512]{4,2,1,3,0:T(8,128)S(1)} %bitcast.142), kind=kOutput, calls=%fused_computation.88 | convolution fusion | flops 1614282752 | bytes 2097152 | tf_op jit(solution)/shard_map/zxy,zk->kxy/dot_general | solution.py:55
  233.9 5.9 %fusion.43 = f32[512,512]{1,0:T(8,128)S(1)} fusion(f32[2,64,8,1,512]{4,2,1,3,0:T(8,128)S(1)} %bitcast.143), kind=kOutput, calls=%fused_computation.87 | convolution fusion | flops 1614282752 | bytes 2097152 | tf_op jit(solution)/shard_map/zxy,zk->kxy/dot_general | solution.py:55
  239.8 5.7 %fusion.12 = f32[1,512,1,512]{3,1,2,0:T(8,128)S(1)} fusion(f32[512,512]{1,0:T(8,128)S(1)} %fusion.44, f32[2,64,8,1,512]{4,2,1,3,0:T(8,128)S(1)} %bitcast.144), kind=kOutput, calls=%fused_computation.44 | convolution fusion | flops 1614544896 | bytes 3145728 | tf_op jit(solution)/shard_map/zxy,zk->kxy/dot_general | solution.py:55
  245.5 6.1 %fusion.13 = f32[1,512,1,512]{3,1,2,0:T(8,128)S(1)} fusion(f32[512,512]{1,0:T(8,128)S(1)} %fusion.43, f32[2,64,8,1,512]{4,2,1,3,0:T(8,128)S(1)} %bitcast.145), kind=kOutput, calls=%fused_computation.46 | convolution fusion | flops 1614544896 | bytes 3145728 | tf_op jit(solution)/shard_map/zxy,zk->kxy/dot_general | solution.py:55
  252.0 5.7 %fusion.46 = f32[512,512]{1,0:T(8,128)S(1)} fusion(f32[2,512,1,512]{3,1,2,0:T(8,128)S(1)} %maximum_multiply_fusion), kind=kOutput, calls=%fused_computation.90 | convolution fusion | flops 1614544896 | bytes 2097152 | tf_op jit(solution)/shard_map/kxy,zk->zxy/dot_general | solution.py:55
  257.8 5.7 %fusion.45 = f32[512,512]{1,0:T(8,128)S(1)} fusion(f32[2,512,1,512]{3,1,2,0:T(8,128)S(1)} %maximum_multiply_fusion), kind=kOutput, calls=%fused_computation.89 | convolution fusion | flops 1614544896 | bytes 2097152 | tf_op jit(solution)/shard_map/kxy,zk->zxy/dot_general | solution.py:55
  263.5 5.9 %fusion.10 = f32[1,512,1,512]{3,1,2,0:T(8,128)S(1)} fusion(f32[512,512]{1,0:T(8,128)S(1)} %fusion.46, f32[2,512,1,512]{3,1,2,0:T(8,128)S(1)} %maximum_multiply_fusion), kind=kOutput, calls=%fused_computation.40 | convolution fusion | flops 1614807040 | bytes 3145728 | tf_op jit(solution)/shard_map/kxy,zk->zxy/dot_general | solution.py:55
  269.4 5.8 %fusion.11 = f32[1,512,1,512]{3,1,2,0:T(8,128)S(1)} fusion(f32[512,512]{1,0:T(8,128)S(1)} %fusion.45, f32[2,512,1,512]{3,1,2,0:T(8,128)S(1)} %maximum_multiply_fusion), kind=kOutput, calls=%fused_computation.42 | convolution fusion | flops 1614807040 | bytes 3145728 | tf_op jit(solution)/shard_map/kxy,zk->zxy/dot_general | solution.py:55
  275.4 3.9 copy.50
  279.3 5.8 %all-to-all-start.2 = ((f32[2,512,1,512]{3,2,0,1:T(1,128)}), f32[2,512,1,512]{3,2,0,1:T(1,128)S(1)}, u32[]{:S(2)}, u32[]{:S(2)}) async-start(f32[2,512,1,512]{3,2,0,1:T(1,128)} %copy.50), calls=%async_computation.2 | async-start | bytes 4194304 | tf_op jit(solution)/shard_map/all_to_all | solution.py:137
  285.2 51.2 %all-to-all-done.2 = f32[2,512,1,512]{3,2,0,1:T(1,128)S(1)} async-done(((f32[2,512,1,512]{3,2,0,1:T(1,128)}), f32[2,512,1,512]{3,2,0,1:T(1,128)S(1)}, u32[]{:S(2)}, u32[]{:S(2)}) %all-to-all-start.2) | async-done | bytes 2097184 | tf_op jit(solution)/shard_map/all_to_all | solution.py:137
  336.8 1.2 copy.69
  338.0 6.6 %fusion.24 = f32[8,64,532]{2,1,0:T(8,128)S(1)} fusion(f32[2,8,64,1,512]{4,2,1,3,0:T(8,128)S(1)} %bitcast.138, s32[532]{0:T(1024)S(1)} %add_select_fusion.4), kind=kOutput, calls=%fused_computation.59 | convolution fusion | flops 1677613056 | bytes 2142208 | tf_op jit(solution)/shard_map/zxk,yk->zxy/dot_general | solution.py:55
  344.6 6.8 %fusion.26 = f32[8,64,532]{2,1,0:T(8,128)S(1)} fusion(f32[2,8,64,1,512]{4,2,1,3,0:T(8,128)S(1)} %bitcast.139, s32[532]{0:T(1024)S(1)} %add_select_fusion.4), kind=kOutput, calls=%fused_computation.61 | convolution fusion | flops 1677613056 | bytes 2142208 | tf_op jit(solution)/shard_map/zxk,yk->zxy/dot_general | solution.py:55
  351.4 6.7 %fusion.5 = f32[1,8,64,532]{3,2,1,0:T(8,128)S(1)} fusion(f32[8,64,532]{2,1,0:T(8,128)S(1)} %fusion.24, f32[2,8,64,1,512]{4,2,1,3,0:T(8,128)S(1)} %bitcast.140, s32[532]{0:T(1024)S(1)} %add_select_fusion.4), kind=kOutput, calls=%fused_computation.33 | convolution fusion | flops 1677885440 | bytes 3452928 | tf_op jit(solution)/shard_map/zxk,yk->zxy/dot_general | solution.py:55
  358.1 6.9 %fusion.6 = f32[1,8,64,532]{3,2,1,0:T(8,128)S(1)} fusion(f32[8,64,532]{2,1,0:T(8,128)S(1)} %fusion.26, f32[2,8,64,1,512]{4,2,1,3,0:T(8,128)S(1)} %bitcast.141, s32[532]{0:T(1024)S(1)} %add_select_fusion.4), kind=kOutput, calls=%fused_computation.35 | convolution fusion | flops 1677885440 | bytes 3452928 | tf_op jit(solution)/shard_map/zxk,yk->zxy/dot_general | solution.py:55
  365.2 4.5 copy.53
  369.7 5.6 %reshape.251 = f32[4,1,136192]{2,1,0:T(1,128)} reshape(f32[532,2,8,64]{3,2,1,0:T(8,128)} %bitcast.134) | data formatting | bytes 4358144
  375.4 3.6 all-to-all-start.3
  379.0 26.9 %all-to-all-done.3 = f32[4,1,136192]{2,1,0:T(1,128)S(1)} async-done(((f32[4,1,136192]{2,1,0:T(1,128)}), f32[4,1,136192]{2,1,0:T(1,128)S(1)}, u32[]{:S(2)}, u32[]{:S(2)}) %all-to-all-start.3) | async-done | bytes 2179104 | tf_op jit(solution)/shard_map/all_to_all | solution.py:140
  405.9 1.4 copy-done
  407.8 7.5 %reduce = f32[4,136192]{1,0:T(4,128)S(1)} reduce(f32[4,1,136192]{2,1,0:T(1,128)} %copy-done, f32[]{:T(128)} %broadcast.1634), dimensions={1}, to_apply=%all_to_all.53.reduce_sub_computation | reduce | bytes 4358148 | tf_op jit(solution)/shard_map/all_to_all | solution.py:140
  415.3 3.6 reshape.252
  418.9 3.9 copy.68
  422.9 2.4 fusion.207
  425.2 2.9 squeeze.19
  428.2 2.2 squeeze.20
  430.3 4.1 fusion.17
  434.4 4.2 convolution_subtract_fusion
  438.8 1.5 collective-permute-start.1
  440.3 16.7 %collective-permute-done.1 = f32[5,133,512]{2,1,0:T(8,128)S(1)} collective-permute-done((f32[5,133,512]{2,1,0:T(8,128)S(1)}, f32[5,133,512]{2,1,0:T(8,128)S(1)}, u32[]{:S(2)}, u32[]{:S(2)}) %collective-permute-start.1) | collective-permute-done | bytes 1361952 | tf_op jit(solution)/shard_map/ppermute | solution.py:19
  457.0 3.2 multiply_reduce_fusion.2
  460.2 3.0 multiply_reduce_fusion
  (73 shorter events, 17.5 us)
Async XLA Ops:
  11.7 0.6 copy-start.10
  13.3 0.7 copy-start.7
  17.1 0.8 copy-start.3
  26.8 18.9 %collective-permute-start = (f32[5,133,512]{2,1,0:T(8,128)}, f32[5,133,512]{2,1,0:T(8,128)}, u32[]{:S(2)}, u32[]{:S(2)}) collective-permute-start(f32[5,133,512]{2,1,0:T(8,128)} %slice.114), channel_id=1, source_target_pairs={{252,0},{0,4},{4,8},{8,12},{12,16},{16,20},{20,24},{24,28},{28,32}... | collective-permute-start | bytes 4085768 | tf_op jit(solution)/shard_map/ppermute | solution.py:19
  31.0 2.3 copy-start.1
  33.4 14.0 %copy-start.6 = (f32[3,133,512]{2,1,0:T(8,128)S(1)}, f32[3,133,512]{2,1,0:T(8,128)}, u32[]{:S(2)}) copy-start(f32[3,133,512]{2,1,0:T(8,128)} %slice.116) | copy-start | bytes 2451460
  136.3 6.3 %copy-start.15 = (f32[8,64,512]{2,1,0:T(8,128)S(1)}, f32[8,64,512]{2,1,0:T(8,128)}, u32[]{:S(2)}) copy-start(f32[8,64,512]{2,1,0:T(8,128)} %fusion.36) | copy-start | bytes 3145732
  142.6 6.8 %copy-start.5 = (f32[8,64,512]{2,1,0:T(8,128)S(1)}, f32[8,64,512]{2,1,0:T(8,128)}, u32[]{:S(2)}) copy-start(f32[8,64,512]{2,1,0:T(8,128)} %squeeze.16) | copy-start | bytes 3145732
  158.6 69.5 %all-to-all-start.1 = ((f32[2,8,64,512]{3,1,0,2:T(8,128)}), f32[2,8,64,512]{3,1,0,2:T(8,128)S(1)}, u32[]{:S(2)}, u32[]{:S(2)}) async-start(f32[2,8,64,512]{3,1,0,2:T(8,128)} %copy.48), calls=%async_computation.1 | async-start | bytes 4194304 | tf_op jit(solution)/shard_map/all_to_all | solution.py:132
  279.3 57.1 %all-to-all-start.2 = ((f32[2,512,1,512]{3,2,0,1:T(1,128)}), f32[2,512,1,512]{3,2,0,1:T(1,128)S(1)}, u32[]{:S(2)}, u32[]{:S(2)}) async-start(f32[2,512,1,512]{3,2,0,1:T(1,128)} %copy.50), calls=%async_computation.2 | async-start | bytes 4194304 | tf_op jit(solution)/shard_map/all_to_all | solution.py:137
  375.4 30.5 %all-to-all-start.3 = ((f32[4,1,136192]{2,1,0:T(1,128)}), f32[4,1,136192]{2,1,0:T(1,128)S(1)}, u32[]{:S(2)}, u32[]{:S(2)}) async-start(f32[4,1,136192]{2,1,0:T(1,128)} %reshape.251), calls=%async_computation.3 | async-start | bytes 4358144 | tf_op jit(solution)/shard_map/all_to_all | solution.py:140
  405.9 1.4 copy-start
  430.3 4.1 copy-start.2
  438.7 18.3 %copy-start.4 = (f32[512,256]{1,0:T(8,128)S(1)}, f32[512,256]{1,0:T(8,128)}, u32[]{:S(2)}) copy-start(f32[512,256]{1,0:T(8,128)} %copy-done.3) | copy-start | bytes 1572868
  438.7 18.3 %copy-start.8 = (f32[133,256]{1,0:T(8,128)S(1)}, f32[133,256]{1,0:T(8,128)}, u32[]{:S(2)}) copy-start(f32[133,256]{1,0:T(8,128)} %copy-done.7) | copy-start | bytes 408580
  438.7 18.3 %copy-start.12 = (f32[133,256]{1,0:T(8,128)S(1)}, f32[133,256]{1,0:T(8,128)}, u32[]{:S(2)}) copy-start(f32[133,256]{1,0:T(8,128)} %get-tuple-element.11) | copy-start | bytes 408580
  438.8 18.2 %collective-permute-start.1 = (f32[5,133,512]{2,1,0:T(8,128)S(1)}, f32[5,133,512]{2,1,0:T(8,128)S(1)}, u32[]{:S(2)}, u32[]{:S(2)}) collective-permute-start(f32[5,133,512]{2,1,0:T(8,128)S(1)} %slice.149), channel_id=1, source_target_pairs={{4,0},{8,4},{12,8},{16,12},{20,16},{24,20},{28,24},{32,28},{36,32}... | collective-permute-start | bytes 4085768 | tf_op jit(solution)/shard_map/ppermute | solution.py:19
  457.0 3.2 copy-start.9
  460.2 3.1 copy-start.11
  460.2 3.1 copy-start.13
  460.2 3.1 copy-start.14
where the time goes:
time: 470 us; the launch traced here: 464 us
  waiting for transfers between devices  157 us (33%)
  matrix products  127 us (27%)
  local copies, waits for them, and re-layouts  70.3 us (15%)
  blocking collectives  48 us (10%)
  starting transfers between devices  32.5 us (7%)
  other arithmetic  27.6 us (6%)
    dot_general x23, matrix products, einsum_high(): jnp.einsum(form, left_arr, right_arr, precision=lax.Precision.HIGHEST)  127 us
    all_to_all x1, waiting for transfers between devices, local(): lax.all_to_all(spectrum, 'gz', split_axis=1, concat_axis=2, tiled=True)  51.2 us
    all_to_all x1, waiting for transfers between devices, local(): lax.all_to_all(spectrum, 'gz', split_axis=2, concat_axis=1, tiled=True)  49.8 us
    all_to_all x1, blocking collectives, local(): lax.all_to_all(spectrum, 'gy', split_axis=2, concat_axis=3, tiled=True)  48 us
    ppermute x2, waiting for transfers between devices, from_behind(): return lax.ppermute(block, axis, route)  29 us
    all_to_all x1, waiting for transfers between devices, local(): lax.all_to_all(spectrum, 'gy', split_axis=3, concat_axis=2, tiled=True)  26.9 us
    all_to_all x1, starting transfers between devices, local(): lax.all_to_all(spectrum, 'gz', split_axis=2, concat_axis=1, tiled=True)  18.4 us
    unnamed x35, local copies, waits for them, and re-layouts  14.1 us
  transfers between devices with their start and end apart: 5, of which 5 were waited for; matrix products, arithmetic and copies ran while one was open for 1% of the time, Pallas kernels for 0%

commit v1 on v0

v1 whole, which is shorter than its diff:
```python
import functools
import math

import jax
import jax.numpy as jnp
import ml_dtypes
import numpy as np
from jax import lax
from jax.experimental import pallas as pl
from jax.experimental.pallas import tpu as pltpu
from jax.sharding import PartitionSpec as P

N = 512
ORDER = 6
BLOCKS = 256
SLOTS = 256
CZ = 8
CY = 128
F32 = jnp.float32
BF16 = jnp.bfloat16
MESH = pl.DeviceIdType.MESH

QXR, QXI, WZ, ZB, YB, DWZ, WY, DWY, P1R, P1I, P2R, P2I, ROWS = (
    0, 6, 12, 18, 19, 20, 26, 32, 38, 39, 40, 41, 42)


def halves(table):
    hi = table.astype(ml_dtypes.bfloat16)
    lo = (table - hi.astype(np.float64)).astype(ml_dtypes.bfloat16)
    return np.stack([hi, lo])


def tables():
    i = np.arange(128)
    ang = 2.0 * np.pi * (np.outer(i, i) % 128) / 128.0
    c, s = np.cos(ang), np.sin(ang)
    fwd_right = np.block([[c, -s], [s, c]])
    inv_right = np.block([[c, s], [-s, c]])
    mats = np.stack([halves(fwd_right), halves(inv_right), halves(fwd_right.T), halves(inv_right.T)])
    tw = 2.0 * np.pi * np.outer(np.arange(4), i) / 512.0
    twy = np.stack([np.cos(tw), np.sin(tw)]).astype(np.float32)
    twz = np.ascontiguousarray(np.broadcast_to(twy[..., None], (2, 4, 128, 128)))
    return mats, twy, twz


def spline_six(t):
    values = [jnp.ones_like(t)]
    slopes = None
    for k in range(2, ORDER + 1):
        prev = values
        if k == ORDER:
            slopes = [
                (prev[j - 1] if j > 0 else 0.0) - (prev[j] if j < k - 1 else 0.0) for j in range(k)
            ]
        values = []
        for j in range(k):
            term = None
            if j > 0:
                term = (t + (k - 1 - j)) * prev[j - 1]
            if j < k - 1:
                upper = ((1.0 + j) - t) * prev[j]
                term = upper if term is None else term + upper
            values.append(term)
    return [v * (1.0 / 120.0) for v in values], [s * (1.0 / 24.0) for s in slopes]


def split(x):
    hi = x.astype(BF16)
    return hi, (x - hi.astype(F32)).astype(BF16)


def mm(a, b):
    return jnp.dot(a, b, preferred_element_type=F32)


def radix4(xr, xi, sign):
    er, ei = xr[0] + xr[2], xi[0] + xi[2]
    dr, di = xr[0] - xr[2], xi[0] - xi[2]
    fr, fi = xr[1] + xr[3], xi[1] + xi[3]
    gr, gi = xr[1] - xr[3], xi[1] - xi[3]
    jr, ji = (gi, -gr) if sign < 0 else (-gi, gr)
    return [er + fr, dr + jr, er - fr, dr - jr], [ei + fi, di + ji, ei - fi, di - ji]


def main_kernel(kx_ref, coef_ref, at_a, at_b, infl, mats, twy, twz, out,
                prep, wzd, dwzd, iota, stage, carry, rolled, hs, grid, spec):
    kx = kx_ref[0]
    eye = lax.broadcasted_iota(jnp.int32, (CY, SLOTS), 0).astype(F32).astype(BF16)
    iota[...] = eye

    def prepare(i, _):
        def comp(j):
            return jnp.concatenate(
                [half[pl.ds(64 * i + j, 8, stride=8), :] for half in (at_a, at_b)], axis=1)

        def put(k, v):
            prep[k, pl.ds(8 * i, 8), :] = v

        q = comp(0)
        wz, dwz = spline_six(comp(4))
        wy, dwy = spline_six(comp(5))
        wx, dwx = spline_six(comp(6))
        m = (comp(3).astype(jnp.int32) * kx) & 511
        quad = (m + 64) >> 7
        f = (m - (quad << 7)).astype(F32) * (math.pi / 256.0)
        f2 = f * f
        sn = f * (1.0 + f2 * (-1.0 / 6 + f2 * (1.0 / 120 + f2 * (-1.0 / 5040 + f2 * (1.0 / 362880)))))
        cs = 1.0 + f2 * (-0.5 + f2 * (1.0 / 24 + f2 * (-1.0 / 720 + f2 * (1.0 / 40320))))
        odd = (quad & 1) == 1
        ca = jnp.where(odd, sn, cs)
        sa = jnp.where(odd, cs, sn)
        ca = jnp.where(((quad + 1) & 2) == 2, -ca, ca)
        sa = jnp.where((quad & 2) == 2, -sa, sa)

        def wave(w):
            br = w[0] * 1.0
            bi = None
            for c in range(1, ORDER):
                br = br + w[c] * coef_ref[c]
                term = w[c] * coef_ref[8 + c]
                bi = term if bi is None else bi + term
            return br * ca - bi * sa, -(br * sa + bi * ca)

        ar, ai = wave(wx)
        dr, di = wave(dwx)
        ar, ai = q * ar, q * ai
        scale = -coef_ref[6]
        qs = q * scale
        put(P1R, ar * scale)
        put(P1I, ai * scale)
        put(P2R, dr * qs)
        put(P2I, di * qs)
        for b in range(ORDER):
            put(QXR + b, ar * wy[b])
            put(QXI + b, ai * wy[b])
            put(WZ + b, wz[b])
            put(DWZ + b, dwz[b])
            put(WY + b, wy[b])
            put(DWY + b, dwy[b])
        put(ZB, comp(1))
        put(YB, comp(2))
        return 0

    lax.fori_loop(0, BLOCKS // 8, prepare, 0)

    def row(k, blk):
        return prep[k, pl.ds(blk, 1), :]

    def one_hot(blk):
        yb = row(YB, blk).astype(BF16)
        return jnp.where(iota[...] == yb, jnp.ones((), BF16), jnp.zeros((), BF16))

    planes = lax.broadcasted_iota(jnp.int32, (16, SLOTS), 0).astype(F32)
    carry[...] = jnp.zeros_like(carry)

    def spread_slab(g, _):
        for h in range(4):
            blk = 4 * g + h
            hot = one_hot(blk)
            d = planes - row(ZB, blk)
            w = jnp.zeros((16, SLOTS), F32)
            dw = w
            for b in range(ORDER):
                hit = d == b
                w = jnp.where(hit, row(WZ + b, blk), w)
                dw = jnp.where(hit, row(DWZ + b, blk), dw)
            wzd[pl.ds(16 * blk, 16), :] = w
            dwzd[pl.ds(16 * blk, 16), :] = dw
            left = jnp.concatenate([row(QXR + k, blk) * w for k in range(12)], axis=0)
            hi, lo = split(left)
            dims = (((1,), (1,)), ((), ()))
            m = lax.dot_general(hi, hot, dims, preferred_element_type=F32)
            m = m + lax.dot_general(lo, hot, dims, preferred_element_type=F32)
            stage[:, h * 128:(h + 1) * 128] = m
        for c in range(2):
            tot = None
            for b in range(ORDER):
                k = 6 * c + b
                t = stage[16 * k:16 * k + 8, :] + carry[8 * k:8 * k + 8, :]
                carry[8 * k:8 * k + 8, :] = stage[16 * k + 8:16 * k + 16, :]
                if b:
                    t = pltpu.roll(t, b, 1)
                tot = t if tot is None else tot + t
            grid[c, pl.ds(pl.multiple_of(8 * g, 8), 8), :] = tot
        return 0

    lax.fori_loop(0, 64, spread_slab, 0)
    for c in range(2):
        tot = grid[c, 0:8, :]
        for b in range(ORDER):
            t = carry[8 * (6 * c + b):8 * (6 * c + b) + 8, :]
            tot = tot + (pltpu.roll(t, b, 1) if b else t)
        grid[c, 0:8, :] = tot

    YR = 64

    def fwd_y(i, _):
        rows = pl.ds(pl.multiple_of(i * YR, YR), YR)
        xr = [grid[0, rows, m * 128:(m + 1) * 128] for m in range(4)]
        xi = [grid[1, rows, m * 128:(m + 1) * 128] for m in range(4)]
        ar, ai = radix4(xr, xi, -1)
        for r in range(4):
            if r:
                c, s = twy[0, r:r + 1, :], twy[1, r:r + 1, :]
                ar[r], ai[r] = ar[r] * c + ai[r] * s, ai[r] * c - ar[r] * s
            hi, lo = split(jnp.concatenate([ar[r], ai[r]], axis=1))
            spec[rows, r * 256:(r + 1) * 256] = (
                mm(hi, mats[0, 0]) + mm(lo, mats[0, 0]) + mm(hi, mats[0, 1]))
        return 0

    lax.fori_loop(0, N // YR, fwd_y, 0)

    def left_mm(which, x):
        hi, lo = split(x)
        return mm(mats[which, 0], hi) + mm(mats[which, 1], hi) + mm(mats[which, 0], lo)

    for rp in range(2):
        base = rp * 512

        def lanes(part):
            return [slice(base + rr * 256 + part * 128, base + rr * 256 + part * 128 + 128) for rr in range(2)]

        def grab(m, part):
            return jnp.concatenate([spec[m * 128:(m + 1) * 128, l] for l in lanes(part)], axis=1)

        xr = [grab(m, 0) for m in range(4)]
        xi = [grab(m, 1) for m in range(4)]
        ar, ai = radix4(xr, xi, -1)
        for s_ in range(4):
            cc = jnp.concatenate([twz[0, s_]] * 2, axis=1)
            ss = jnp.concatenate([twz[1, s_]] * 2, axis=1)
            if s_:
                ar[s_], ai[s_] = ar[s_] * cc + ai[s_] * ss, ai[s_] * cc - ar[s_] * ss
            f = left_mm(2, jnp.concatenate([ar[s_], ai[s_]], axis=0))
            w = infl[s_ * 128:(s_ + 1) * 128, rp * 256:(rp + 1) * 256]
            f = f * jnp.concatenate([w, w], axis=0)
            f = left_mm(3, f)
            ur, ui = f[:128], f[128:]
            if s_:
                ur, ui = ur * cc - ui * ss, ui * cc + ur * ss
            ar[s_], ai[s_] = ur, ui
        br, bi = radix4(ar, ai, 1)
        for m in range(4):
            for part, v in ((0, br[m]), (1, bi[m])):
                for rr, l in enumerate(lanes(part)):
                    spec[m * 128:(m + 1) * 128, l] = v[:, rr * 128:(rr + 1) * 128]

    def inv_y(i, _):
        rows = pl.ds(pl.multiple_of(i * YR, YR), YR)
        ar, ai = [], []
        for r in range(4):
            hi, lo = split(spec[rows, r * 256:(r + 1) * 256])
            x = mm(hi, mats[1, 0]) + mm(lo, mats[1, 0]) + mm(hi, mats[1, 1])
            ur, ui = x[:, :128], x[:, 128:]
            if r:
                c, s = twy[0, r:r + 1, :], twy[1, r:r + 1, :]
                ur, ui = ur * c - ui * s, ui * c + ur * s
            ar.append(ur)
            ai.append(ui)
        br, bi = radix4(ar, ai, 1)
        for m in range(4):
            grid[0, rows, m * 128:(m + 1) * 128] = br[m]
            grid[1, rows, m * 128:(m + 1) * 128] = bi[m]
        return 0

    lax.fori_loop(0, N // YR, inv_y, 0)

    def roll_tile(tile, c, b):
        t = grid[c, pl.ds(pl.multiple_of(8 * tile, 8), 8), :]
        return pltpu.roll(t, N - b, 1) if b else t

    for c in range(2):
        for b in range(ORDER):
            rolled[8 * (6 * c + b):8 * (6 * c + b) + 8, :] = roll_tile(0, c, b)

    def gather_slab(g, _):
        nxt = (g + 1) & 63
        for c in range(2):
            for b in range(ORDER):
                k = 6 * c + b
                t = roll_tile(nxt, c, b)
                hi, lo = split(jnp.concatenate([rolled[8 * k:8 * k + 8, :], t], axis=0))
                rolled[8 * k:8 * k + 8, :] = t
                for h in range(4):
                    hs[16 * k:16 * k + 16, h * 256:h * 256 + 128] = hi[:, h * 128:(h + 1) * 128]
                    hs[16 * k:16 * k + 16, h * 256 + 128:h * 256 + 256] = lo[:, h * 128:(h + 1) * 128]
        for h in range(4):
            blk = 4 * g + h
            hot = one_hot(blk)
            v = mm(hs[:, h * 256:(h + 1) * 256], jnp.concatenate([hot, hot], axis=0))
            a, s = [], []
            for c in range(2):
                wsum = ssum = None
                for b in range(ORDER):
                    part = v[16 * (6 * c + b):16 * (6 * c + b) + 16, :]
                    wt, st = part * row(WY + b, blk), part * row(DWY + b, blk)
                    wsum = wt if wsum is None else wsum + wt
                    ssum = st if ssum is None else ssum + st
                a.append(wsum)
                s.append(ssum)
            p1r, p1i, p2r, p2i = (row(k, blk) for k in (P1R, P1I, P2R, P2I))
            w = wzd[pl.ds(16 * blk, 16), :]
            dw = dwzd[pl.ds(16 * blk, 16), :]
            fz = jnp.sum(dw * (p1r * a[0] + p1i * a[1]), axis=0, keepdims=True)
            fy = jnp.sum(w * (p1r * s[0] + p1i * s[1]), axis=0, keepdims=True)
            fx = jnp.sum(w * (p2r * a[0] + p2i * a[1]), axis=0, keepdims=True)
            for d, f in enumerate((fz, fy, fx)):
                for half in range(2):
                    out[blk, pl.ds(2 * d + half, 1), :] = f[:, half * 128:(half + 1) * 128]
            out[blk, 6:8, :] = jnp.zeros((2, 128), F32)
        return 0

    lax.fori_loop(0, 64, gather_slab, 0)


def run_main(kx, coef, at_a, at_b, infl):
    mats, twy, twz = tables()
    vm = pl.BlockSpec(memory_space=pltpu.VMEM)
    sm = pl.BlockSpec(memory_space=pltpu.SMEM)
    return pl.pallas_call(
        main_kernel,
        out_shape=jax.ShapeDtypeStruct((BLOCKS, 8, 128), F32),
        in_specs=[sm, sm, vm, vm, vm, vm, vm, vm],
        out_specs=vm,
        scratch_shapes=[
            pltpu.VMEM((ROWS, BLOCKS, SLOTS), F32),
            pltpu.VMEM((BLOCKS * 16, SLOTS), F32),
            pltpu.VMEM((BLOCKS * 16, SLOTS), F32),
            pltpu.VMEM((CY, SLOTS), BF16),
            pltpu.VMEM((192, N), F32),
            pltpu.VMEM((96, N), F32),
            pltpu.VMEM((96, N), F32),
            pltpu.VMEM((192, 2 * N), BF16),
            pltpu.VMEM((2, N, N), F32),
            pltpu.VMEM((N, 2 * N), F32),
        ],
        compiler_params=pltpu.CompilerParams(vmem_limit_bytes=56 * 1024 * 1024),
        cost_estimate=pl.CostEstimate(flops=60_000_000_000, bytes_accessed=6_000_000, transcendentals=0),
    )(kx, coef, at_a, at_b, infl, jnp.asarray(mats), jnp.asarray(twy), jnp.asarray(twz))


def place():
    gz = lax.axis_index("gz")
    return gz // 16, (gz // 2) % 8, gz % 2, lax.axis_index("gy")


def device(x, z, c, y):
    return {"gz": x * 16 + z * 2 + c, "gy": y}


def peers():
    x, z, c, y = place()
    yield device(x, z, 1 - c, y)
    for k in range(1, 4):
        yield device((x + k) % 4, z, c, y)
        yield device(x, z, c, (y + k) % 4)
    for k in range(1, 8):
        yield device(x, (z + k) % 8, c, y)


def meet():
    barrier = pltpu.get_barrier_semaphore()
    for peer in peers():
        pl.semaphore_signal(barrier, inc=1, device_id=peer, device_id_type=MESH)
    pl.semaphore_wait(barrier, 14)


def send(src, dst, sems, k, to):
    copy = pltpu.make_async_remote_copy(
        src_ref=src, dst_ref=dst, send_sem=sems.at[0, k], recv_sem=sems.at[1, k],
        device_id=to, device_id_type=MESH)
    copy.start()
    return copy


def gather_kernel(mine, half_a, half_b, sems):
    x, z, c, y = place()
    cy = c * 4 + y
    meet()
    half_a[x, z, cy] = mine[0:8, :]
    half_b[x, z, cy] = mine[8:16, :]
    flying = []

    def go(ref, to, k):
        flying.append(send(ref, ref, sems, k, to))

    def landed(ref, k):
        pltpu.make_async_remote_copy(
            src_ref=ref, dst_ref=ref, send_sem=sems.at[0, k], recv_sem=sems.at[1, k],
            device_id=device(x, z, 1 - c, y), device_id_type=MESH).wait_recv()

    for k in range(1, 8):
        to = device(x, (z + k) % 8, c, y)
        go(half_a.at[x, z, cy], to, k)
        go(half_b.at[x, z, cy], to, 8 + k)
    for k in range(1, 8):
        landed(half_a.at[x, (z + 8 - k) % 8, cy], k)
        landed(half_b.at[x, (z + 8 - k) % 8, cy], 8 + k)
    for k in range(1, 4):
        go(half_a.at[x, :, cy], device((x + k) % 4, z, c, y), 16 + k)
        go(half_b.at[x, :, cy], device(x, z, c, (y + k) % 4), 20 + k)
    for k in range(1, 4):
        landed(half_a.at[(x + 4 - k) % 4, :, cy], 16 + k)
        landed(half_b.at[x, :, c * 4 + (y + 4 - k) % 4], 20 + k)
    for k in range(1, 4):
        go(half_a.at[:, :, cy], device(x, z, c, (y + k) % 4), 24 + k)
        go(half_b.at[x, :, pl.ds(c * 4, 4)], device((x + k) % 4, z, c, y), 28 + k)
    for k in range(1, 4):
        landed(half_a.at[:, :, c * 4 + (y + 4 - k) % 4], 24 + k)
        landed(half_b.at[(x + 4 - k) % 4, :, pl.ds(c * 4, 4)], 28 + k)
    go(half_a.at[:, :, pl.ds(c * 4, 4)], device(x, z, 1 - c, y), 0)
    go(half_b.at[:, :, pl.ds(c * 4, 4)], device(x, z, 1 - c, y), 8)
    landed(half_a.at[:, :, pl.ds(4 - c * 4, 4)], 0)
    landed(half_b.at[:, :, pl.ds(4 - c * 4, 4)], 8)
    for copy in flying:
        copy.wait_send()


def gather_atoms(mine):
    vm = pl.BlockSpec(memory_space=pltpu.VMEM)
    shape = jax.ShapeDtypeStruct((4, 8, 8, 8, 128), F32)
    return pl.pallas_call(
        gather_kernel, out_shape=(shape, shape), in_specs=[vm], out_specs=(vm, vm),
        scratch_shapes=[pltpu.SemaphoreType.DMA((2, 32))],
        compiler_params=pltpu.CompilerParams(collective_id=0, has_side_effects=True),
    )(mine)


def scatter_kernel(full, out, r0, s0, r1a, r1b, s1a, s1b, r2, s2, r3, sems):
    x, z, c, y = place()
    meet()
    flying = []

    def go(src, dst, to, k):
        flying.append(send(src, dst, sems, k, to))

    def landed(dst, k):
        pltpu.make_async_remote_copy(
            src_ref=dst, dst_ref=dst, send_sem=sems.at[0, k], recv_sem=sems.at[1, k],
            device_id=device(x, z, 1 - c, y), device_id_type=MESH).wait_recv()

    go(full.at[:, :, pl.ds(4 - c * 4, 4)], r0, device(x, z, 1 - c, y), 0)
    landed(r0, 0)
    s0[...] = full[:, :, pl.ds(c * 4, 4)] + r0[...]
    for k in range(1, 4):
        xk, yk = (x + k) % 4, (y + k) % 4
        go(s0.at[xk, 0:4], r1a.at[k], device(xk, z, c, y), k)
        go(s0.at[:, 4:8, yk], r1b.at[k], device(x, z, c, yk), 4 + k)
    s1a[...] = s0[x, 0:4]
    s1b[...] = s0[:, 4:8, y]
    for k in range(1, 4):
        landed(r1a.at[k], k)
        landed(r1b.at[k], 4 + k)
    s1a[...] += r1a[1] + r1a[2] + r1a[3]
    s1b[...] += r1b[1] + r1b[2] + r1b[3]
    for k in range(1, 4):
        xk, yk = (x + k) % 4, (y + k) % 4
        go(s1a.at[:, yk], r2.at[0, k], device(x, z, c, yk), 8 + k)
        go(s1b.at[xk], r2.at[1, k], device(xk, z, c, y), 12 + k)
    for k in range(1, 4):
        landed(r2.at[0, k], 8 + k)
        landed(r2.at[1, k], 12 + k)
    s2[0:4] = s1a[:, y] + r2[0, 1] + r2[0, 2] + r2[0, 3]
    s2[4:8] = s1b[x] + r2[1, 1] + r2[1, 2] + r2[1, 3]
    for k in range(1, 8):
        zk = (z + k) % 8
        go(s2.at[zk], r3.at[k], device(x, zk, c, y), 16 + k)
    total = s2[z]
    for k in range(1, 8):
        landed(r3.at[k], 16 + k)
    for k in range(1, 8):
        total = total + r3[k]
    out[...] = total
    for copy in flying:
        copy.wait_send()


def scatter_forces(full):
    vm = pl.BlockSpec(memory_space=pltpu.VMEM)
    tile = (8, 128)
    return pl.pallas_call(
        scatter_kernel, out_shape=jax.ShapeDtypeStruct(tile, F32), in_specs=[vm], out_specs=vm,
        scratch_shapes=[
            pltpu.VMEM((4, 8, 4) + tile, F32),
            pltpu.VMEM((4, 8, 4) + tile, F32),
            pltpu.VMEM((4, 4, 4) + tile, F32),
            pltpu.VMEM((4, 4, 4) + tile, F32),
            pltpu.VMEM((4, 4) + tile, F32),
            pltpu.VMEM((4, 4) + tile, F32),
            pltpu.VMEM((2, 4, 4) + tile, F32),
            pltpu.VMEM((8,) + tile, F32),
            pltpu.VMEM((8,) + tile, F32),
            pltpu.SemaphoreType.DMA((2, 24)),
        ],
        compiler_params=pltpu.CompilerParams(collective_id=1, has_side_effects=True),
    )(full)


def own_atoms(charges, grid_base, fraction, counts):
    gz, gy = lax.axis_index("gz"), lax.axis_index("gy")
    slots = jnp.arange(SLOTS, dtype=jnp.int32)
    q = jnp.where(slots < counts[0, 0], charges, 0.0)
    base = grid_base - jnp.stack([gz * CZ, gy * CY, 0])[:, None]
    rows = jnp.concatenate(
        [q[None], base.astype(F32), fraction, jnp.zeros((1, SLOTS), F32)], axis=0)
    return rows.reshape(8, 2, 128).transpose(1, 0, 2).reshape(16, 128)


def wave_numbers():
    kx = (lax.axis_index("gy") * 64 + lax.axis_index("gz")).astype(jnp.int32)
    c = jnp.arange(ORDER, dtype=jnp.int32)
    ang = ((c * kx) % N).astype(F32) * (2.0 * math.pi / N)
    scale = jnp.where(kx == 0, 1.0, 2.0).astype(F32) / float(N) ** 3
    coef = jnp.concatenate([jnp.cos(ang), scale[None], jnp.zeros((1,), F32), jnp.sin(ang), jnp.zeros((2,), F32)])
    return kx[None], coef


def local(charges, grid_base, fraction, counts, influence):
    mine = own_atoms(charges, grid_base, fraction, counts)
    at_a, at_b = gather_atoms(mine)
    kx, coef = wave_numbers()
    infl = influence.reshape(128, 4, 128, 4).transpose(1, 0, 3, 2).reshape(N, N)
    part = run_main(kx, coef, at_a.reshape(BLOCKS * 8, 128), at_b.reshape(BLOCKS * 8, 128), infl)
    total = scatter_forces(part.reshape(4, 8, 8, 8, 128))
    return total[:6].reshape(3, SLOTS)


def solution(mesh):
    placed = (
        P(("gz", "gy")),
        P(None, ("gz", "gy")),
        P(None, ("gz", "gy")),
        P("gz", "gy"),
        P(None, ("gy", "gz"), None),
    )
    return jax.shard_map(
        local, mesh=mesh, in_specs=placed, out_specs=P(None, ("gz", "gy")), check_vma=False
    )
```

time: 470 us -> 183 us (0.39); the launches traced: 464 us -> 183 us
  waiting for transfers between devices: 157 us -> 0 us
  matrix products: 127 us -> 0 us
  Pallas kernels: 0 us -> 118 us
  blocking collectives: 48 us -> 0 us
  starting transfers between devices: 32.5 us -> 0 us
  other arithmetic: 27.6 us -> 6.63 us
  local copies, waits for them, and re-layouts: 70.3 us -> 57.1 us
    all_to_all x3 -> x0, waiting for transfers between devices: 128 us -> none  [the longest x1 51.2 us: local(): lax.all_to_all(spectrum, 'gz', split_axis=1, concat_axis=2, tiled=True)]
    dot_general x23 -> x0, matrix products: 127 us -> none  [einsum_high(): jnp.einsum(form, left_arr, right_arr, precision=lax.Precision.HIGHEST)]
    pallas_call x0 -> x3, Pallas kernels: none -> 118 us  [the longest x1 68.7 us: run_main(): pl.pallas_call(main_kernel, out_shape=jax.ShapeDtypeStruct((BLOCKS, 8, 12...]
    all_to_all x1 -> x0, blocking collectives: 48 us -> none  [local(): lax.all_to_all(spectrum, 'gy', split_axis=2, concat_axis=3, tiled=True)]
    reshape x0 -> x2, local copies, waits for them, and re-layouts: none -> 37.2 us  [the longest x1 36 us: local(): infl = influence.reshape(128, 4, 128, 4).transpose(1, 0, 3, 2).reshape(N, N)]
    ppermute x2 -> x0, waiting for transfers between devices: 29 us -> none  [from_behind(): return lax.ppermute(block, axis, route)]
    all_to_all x3 -> x0, starting transfers between devices: 27.8 us -> none  [the longest x1 18.4 us: local(): lax.all_to_all(spectrum, 'gz', split_axis=2, concat_axis=1, tiled=True)]
    slice x12 -> x0, local copies, waits for them, and re-layouts: 18.4 us -> none  [the longest x2 4.38 us: local(): moved = from_behind(spread[planes:], 'gz', 1)]
  transfers between devices with their start and end apart: 5 -> 0, of which waited for: 5 -> 0; matrix products, arithmetic and copies ran while one was open for 1% -> 0% of each run, Pallas kernels for 0% -> 0%
where the time goes in v1:
time: 183 us
  Pallas kernels  118 us (64%)
  local copies, waits for them, and re-layouts  57.1 us (31%)
  other arithmetic  6.63 us (4%)
    pallas_call x1, Pallas kernels, run_main(): pl.pallas_call(main_kernel, out_shape=jax.ShapeDtypeStruct((BLOCKS, 8, 12...  68.7 us
    reshape x1, local copies, waits for them, and re-layouts, local(): infl = influence.reshape(128, 4, 128, 4).transpose(1, 0, 3, 2).reshape(N, N)  36 us
    pallas_call x1, Pallas kernels, gather_atoms(): pl.pallas_call(gather_kernel, out_shape=(shape, shape), in_specs=[vm], ou...  30.7 us
    pallas_call x1, Pallas kernels, scatter_forces(): pl.pallas_call(scatter_kernel, out_shape=jax.ShapeDtypeStruct(tile, F32),...  18.7 us
    transpose x1, local copies, waits for them, and re-layouts, local(): infl = influence.reshape(128, 4, 128, 4).transpose(1, 0, 3, 2).reshape(N, N)  18.1 us
    unnamed x1, other arithmetic  3.72 us

profile of v1, /device:TPU:1, one launch (start us, length us, event | category | flops | bytes accessed | tf_op | source)
XLA Modules:
  0.0 182.5 jit_solution(2349669334120384094)
XLA Ops:
  0.7 0.1 pad_add_fusion
  0.7 0.7 compare_select_fusion.2
  1.4 0.1 pad.3.clone
  1.5 0.1 fusion.3
  1.5 0.6 concatenate.13.coef_ref
  2.2 0.8 convert_bitcast_fusion
  2.9 1.3 maximum_bitcast_fusion.mine
  4.3 3.7 %reduce = f32[512,512]{1,0:T(8,128)S(1)} reduce(f32[512,1,512]{2,1,0:T(1,128)} %param.12, f32[]{:T(128)} %constant.59), dimensions={1}, to_apply=%param.12.reduce_sub_computation | reduce | bytes 2097156 | tf_op args[4]
  8.0 30.7 %shard_map.82 = (f32[4,8,8,8,128]{4,3,2,1,0:T(8,128)}, f32[4,8,8,8,128]{4,3,2,1,0:T(8,128)}) custom-call(f32[16,128]{1,0:T(8,128)} %maximum_bitcast_fusion.mine), custom_call_target="tpu_custom_call" | custom-call | tf_op jit(solution)/shard_map/pallas_call | solution.py:422
  38.6 36.0 %reshape.31 = f32[128,4,128,4]{3,2,1,0:T(8,128)} reshape(f32[512,512]{1,0:T(8,128)S(1)} %reduce) | data formatting | bytes 2097152 | tf_op jit(solution)/shard_map/reshape | solution.py:522
  74.6 18.1 %copy.14 = f32[4,128,4,128]{3,2,1,0:T(4,128)S(1)} copy(f32[4,128,4,128]{2,3,0,1:T(8,128)} %bitcast.25) | data formatting | bytes 2097152 | tf_op jit(solution)/shard_map/transpose | solution.py:522
  92.7 1.1 copy.17
  93.8 68.7 %shard_map.83 = f32[256,8,128]{2,1,0:T(8,128)} custom-call(s32[1]{0:T(128)} %bitcast.kx_ref, f32[16]{0:T(128)} %concatenate.13.coef_ref, f32[2048,128]{1,0:T(8,128)} %bitcast.32, f32[2048,128]{1,0:T(8,128)} %bitcast.33, f32[512,512]{1,0:T(8,128)} %bitcast.27, bf16[4,2,256,256]{3,2,1,0:T(8,128)(2,1)} %constant.54.clone.mats, ...), custom_call_target="tpu_custom_call" | custom-call | flops 60000002048 | bytes 6000000 | tf_op jit(solution)/shard_map/pallas_call | solution.py:320
  162.5 18.7 %shard_map.84 = f32[8,128]{1,0:T(8,128)} custom-call(f32[4,8,8,8,128]{4,3,2,1,0:T(8,128)} %bitcast.28), custom_call_target="tpu_custom_call" | custom-call | tf_op jit(solution)/shard_map/pallas_call | solution.py:481
  181.2 1.3 reshape.34
  (1 shorter events, 0.0 us)

commit v2 on v0

v2 whole, which is shorter than its diff:
```python
import functools
import math

import jax
import jax.numpy as jnp
import ml_dtypes
import numpy as np
from jax import lax
from jax.experimental import pallas as pl
from jax.experimental.pallas import tpu as pltpu
from jax.sharding import PartitionSpec as P

N = 512
ORDER = 6
BLOCKS = 128
SLOTS = 256
SLABS = 32
CZ = 8
CY = 128
F32 = jnp.float32
BF16 = jnp.bfloat16
MESH = pl.DeviceIdType.MESH

QX, P2, WZ, DWZ, WY, DWY, ZB, YL, YT, ROWS = 0, 4, 8, 14, 20, 26, 32, 33, 34, 35


def halves(table):
    hi = table.astype(ml_dtypes.bfloat16)
    lo = (table - hi.astype(np.float64)).astype(ml_dtypes.bfloat16)
    return np.stack([hi, lo])


def tables():
    i = np.arange(128)
    ang = 2.0 * np.pi * (np.outer(i, i) % 128) / 128.0
    c, s = np.cos(ang), np.sin(ang)
    fwd_right = np.block([[c, -s], [s, c]])
    inv_right = np.block([[c, s], [-s, c]])
    mats = np.stack([halves(fwd_right), halves(inv_right), halves(fwd_right.T), halves(inv_right.T)])
    tw = 2.0 * np.pi * np.outer(np.arange(4), i) / 512.0
    twy = np.stack([np.cos(tw), np.sin(tw)]).astype(np.float32)
    twz = np.ascontiguousarray(np.broadcast_to(twy[..., None], (2, 4, 128, 128)))
    return mats, twy, twz


def reorder():
    ky = np.arange(N)
    table = np.zeros((N, N), np.float32)
    table[ky, (ky % 4) * 128 + ky // 4] = 1.0
    return table.astype(ml_dtypes.bfloat16)


def spline_six(t):
    values = [jnp.ones_like(t)]
    slopes = None
    for k in range(2, ORDER + 1):
        prev = values
        if k == ORDER:
            slopes = [
                (prev[j - 1] if j > 0 else 0.0) - (prev[j] if j < k - 1 else 0.0) for j in range(k)
            ]
        values = []
        for j in range(k):
            term = None
            if j > 0:
                term = (t + (k - 1 - j)) * prev[j - 1]
            if j < k - 1:
                upper = ((1.0 + j) - t) * prev[j]
                term = upper if term is None else term + upper
            values.append(term)
    return [v * (1.0 / 120.0) for v in values], [s * (1.0 / 24.0) for s in slopes]


def split(x):
    hi = x.astype(BF16)
    return hi, (x - hi.astype(F32)).astype(BF16)


def mm(a, b):
    return jnp.dot(a, b, preferred_element_type=F32)


def radix4(xr, xi, sign):
    er, ei = xr[0] + xr[2], xi[0] + xi[2]
    dr, di = xr[0] - xr[2], xi[0] - xi[2]
    fr, fi = xr[1] + xr[3], xi[1] + xi[3]
    gr, gi = xr[1] - xr[3], xi[1] - xi[3]
    jr, ji = (gi, -gr) if sign < 0 else (-gi, gr)
    return [er + fr, dr + jr, er - fr, dr - jr], [ei + fi, di + ji, ei - fi, di - ji]


def turn(m):
    m = m & (N - 1)
    quad = (m + 64) >> 7
    f = (m - (quad << 7)).astype(F32) * (math.pi / 256.0)
    f2 = f * f
    sn = f * (1.0 + f2 * (-1.0 / 6 + f2 * (1.0 / 120 + f2 * (-1.0 / 5040 + f2 * (1.0 / 362880)))))
    cs = 1.0 + f2 * (-0.5 + f2 * (1.0 / 24 + f2 * (-1.0 / 720 + f2 * (1.0 / 40320))))
    odd = (quad & 1) == 1
    cos = jnp.where(odd, sn, cs)
    sin = jnp.where(odd, cs, sn)
    cos = jnp.where(((quad + 1) & 2) == 2, -cos, cos)
    sin = jnp.where((quad & 2) == 2, -sin, sin)
    return cos, sin


def place():
    gz = lax.axis_index("gz")
    return gz // 16, (gz // 2) % 8, gz % 2, lax.axis_index("gy")


def device(x, z, c, y):
    return {"gz": x * 16 + z * 2 + c, "gy": y}


def peers():
    x, z, c, y = place()
    yield device(x, z, 1 - c, y)
    for k in range(1, 4):
        yield device((x + k) % 4, z, c, y)
        yield device(x, z, c, (y + k) % 4)
    for k in range(1, 8):
        yield device(x, (z + k) % 8, c, y)


def meet():
    barrier = pltpu.get_barrier_semaphore()
    for peer in peers():
        pl.semaphore_signal(barrier, inc=1, device_id=peer, device_id_type=MESH)
    pl.semaphore_wait(barrier, 14)


def remote(src, dst, sems, k, to):
    return pltpu.make_async_remote_copy(
        src_ref=src, dst_ref=dst, send_sem=sems.at[0, k], recv_sem=sems.at[1, k],
        device_id=to, device_id_type=MESH)


def gather_atoms(half_a, half_b, sems, meanwhile):
    x, z, c, y = place()
    sib = device(x, z, 1 - c, y)
    flying = []

    def go(ref, to, k):
        copy = remote(ref, ref, sems, k, to)
        copy.start()
        flying.append(copy)

    def landed(ref, k):
        remote(ref, ref, sems, k, sib).wait_recv()

    for k in range(1, 8):
        to = device(x, (z + k) % 8, c, y)
        go(half_a.at[x, z, y], to, k)
        go(half_b.at[x, z, y], to, 8 + k)
    meanwhile()
    for k in range(1, 8):
        landed(half_a.at[x, (z + 8 - k) % 8, y], k)
        landed(half_b.at[x, (z + 8 - k) % 8, y], 8 + k)
    for k in range(1, 4):
        go(half_a.at[x, :, y], device((x + k) % 4, z, c, y), 16 + k)
        go(half_b.at[x, :, y], device(x, z, c, (y + k) % 4), 20 + k)
    for k in range(1, 4):
        landed(half_a.at[(x + 4 - k) % 4, :, y], 16 + k)
        landed(half_b.at[x, :, (y + 4 - k) % 4], 20 + k)
    for k in range(1, 4):
        go(half_a.at[:, :, y], device(x, z, c, (y + k) % 4), 24 + k)
        go(half_b.at[x], device((x + k) % 4, z, c, y), 28 + k)
    for k in range(1, 4):
        landed(half_a.at[:, :, (y + 4 - k) % 4], 24 + k)
        landed(half_b.at[(x + 4 - k) % 4], 28 + k)
    for copy in flying:
        copy.wait_send()


def scatter_forces(full, r1a, r1b, s1a, s1b, r2, s2, r3, sems):
    x, z, c, y = place()
    sib = device(x, z, 1 - c, y)
    flying = []

    def go(src, dst, to, k):
        copy = remote(src, dst, sems, k, to)
        copy.start()
        flying.append(copy)

    def landed(dst, k):
        remote(dst, dst, sems, k, sib).wait_recv()

    for k in range(1, 4):
        xk, yk = (x + k) % 4, (y + k) % 4
        go(full.at[xk, 0:4], r1a.at[k], device(xk, z, c, y), k)
        go(full.at[:, 4:8, yk], r1b.at[k], device(x, z, c, yk), 4 + k)
    for k in range(1, 4):
        landed(r1a.at[k], k)
        landed(r1b.at[k], 4 + k)
    s1a[...] = full[x, 0:4] + r1a[1] + r1a[2] + r1a[3]
    s1b[...] = full[:, 4:8, y] + r1b[1] + r1b[2] + r1b[3]
    for k in range(1, 4):
        xk, yk = (x + k) % 4, (y + k) % 4
        go(s1a.at[:, yk], r2.at[0, k], device(x, z, c, yk), 8 + k)
        go(s1b.at[xk], r2.at[1, k], device(xk, z, c, y), 12 + k)
    for k in range(1, 4):
        landed(r2.at[0, k], 8 + k)
        landed(r2.at[1, k], 12 + k)
    s2[0:4] = s1a[:, y] + r2[0, 1] + r2[0, 2] + r2[0, 3]
    s2[4:8] = s1b[x] + r2[1, 1] + r2[1, 2] + r2[1, 3]
    for k in range(1, 8):
        zk = (z + k) % 8
        go(s2.at[zk], r3.at[k], device(x, zk, c, y), 16 + k)
    total = s2[z]
    for k in range(1, 8):
        landed(r3.at[k], 16 + k)
        total = total + r3[k]
    for copy in flying:
        copy.wait_send()
    return total


def main_kernel(counts, charges, base, frac, infl_hbm, perm_hbm, mats_hbm, twy, twz_hbm, out,
                infl, perm, mats, twz, half_a, half_b, coefs, prep, wzd, dwzd, wtab, halo, u, spec,
                filt, hown, hsib, hs_hi, hs_lo, part, r1a, r1b, s1a, s1b, r2, s2, r3,
                local_sems, ag_sems, grid_sems, pot_sems, rs_sems):
    x, z, core, y = place()
    sibling = device(x, z, 1 - core, y)
    gz = lax.axis_index("gz")
    kx = y * 64 + gz
    kxs = (kx, kx + 1 - 2 * core)

    loads = [
        pltpu.make_async_copy(src, dst, local_sems.at[i])
        for i, (src, dst) in enumerate(
            ((infl_hbm, infl), (perm_hbm, perm), (mats_hbm, mats), (twz_hbm, twz)))
    ]
    for load in loads:
        load.start()
    meet()

    for half, ref in enumerate((half_a, half_b)):
        lanes = slice(half * 128, half * 128 + 128)
        slots = lax.broadcasted_iota(jnp.int32, (1, 128), 1) + half * 128
        q = jnp.where(slots < counts[0, 0], charges[half:half + 1, :], 0.0)
        ref[x, z, y] = jnp.concatenate(
            [q, (base[0:1, lanes] - gz * CZ).astype(F32), (base[1:2, lanes] - y * CY).astype(F32),
             base[2:3, lanes].astype(F32), frac[:, lanes], jnp.zeros((1, 128), F32)], axis=0)

    def meanwhile():
        c_rows = lax.broadcasted_iota(jnp.int32, (8, SLOTS), 0)
        for j in range(2):
            cs, sn = turn(c_rows * kxs[j])
            coefs[j, 0] = cs
            coefs[j, 1] = sn
        for load in loads:
            load.wait()
        scale = jnp.where(kx == 0, 1.0, 2.0) / float(N) ** 3
        for s_ in range(4):
            rows = jnp.concatenate(
                [infl[pl.ds(4 * s_ + t, 128, stride=16), :] for t in range(4)], axis=1)
            hi, lo = split(rows * scale)
            filt[s_ * 128:(s_ + 1) * 128, :] = mm(hi, perm[...]) + mm(lo, perm[...])
        halo[...] = jnp.zeros_like(halo)

    gather_atoms(half_a, half_b, ag_sems, meanwhile)
    flat = [half.reshape(BLOCKS * 8, 128) for half in (half_a, half_b)]

    def prepare(i, _):
        def comp(j):
            return jnp.concatenate(
                [half[pl.ds(64 * i + j, 8, stride=8), :] for half in flat], axis=1)

        def put(k, v):
            prep[k, pl.ds(pl.multiple_of(8 * i, 8), 8), :] = v

        q = comp(0)
        wz, dwz = spline_six(comp(4))
        wy, dwy = spline_six(comp(5))
        wx, dwx = spline_six(comp(6))
        wx = [q * w for w in wx]
        dwx = [q * w for w in dwx]
        cell = comp(3).astype(jnp.int32)
        for j in range(2):
            ca, sa = turn(cell * kxs[j])

            def wave(w):
                br = w[0]
                bi = None
                for c in range(1, ORDER):
                    br = br + w[c] * coefs[j, 0, c:c + 1, :]
                    term = w[c] * coefs[j, 1, c:c + 1, :]
                    bi = term if bi is None else bi + term
                return br * ca - bi * sa, -(br * sa + bi * ca)

            for first, w in ((QX, wx), (P2, dwx)):
                re, im = wave(w)
                put(first + 2 * j, re)
                put(first + 2 * j + 1, im)
        for b in range(ORDER):
            put(WZ + b, wz[b])
            put(DWZ + b, dwz[b])
            put(WY + b, wy[b])
            put(DWY + b, dwy[b])
        yb = comp(2).astype(jnp.int32)
        put(ZB, comp(1))
        put(YL, (yb & 15).astype(F32))
        put(YT, (yb >> 4).astype(F32))
        return 0

    lax.fori_loop(0, BLOCKS // 8, prepare, 0)

    def row(k, n):
        return prep[k, pl.ds(n, 1), :]

    planes = lax.broadcasted_iota(jnp.int32, (16, SLOTS), 0).astype(F32)
    bands = lax.broadcasted_iota(jnp.int32, (24, SLOTS), 0).astype(F32)

    def y_tables(n, first):
        d = bands - row(YL, n)
        w = jnp.zeros((24, SLOTS), F32)
        for b in range(ORDER):
            w = jnp.where(d == b, row(first + b, n), w)
        w = jnp.concatenate([w, jnp.zeros((8, SLOTS), F32)], axis=0)
        yt = jnp.broadcast_to(row(YT, n), (16, SLOTS)).astype(BF16)
        hits = [yt == jnp.full((), t, BF16) for t in range(8)]
        zero = jnp.zeros((16, SLOTS), BF16)
        tabs = []
        for v in split(w):
            tiles = []
            for t in range(9):
                tile = jnp.where(hits[t - 1], v[16:], zero) if t else zero
                tiles.append(jnp.where(hits[t], v[:16], tile) if t < 8 else tile)
            tabs.append(jnp.concatenate(tiles, axis=0))
        return tabs

    def nt(a, b):
        return lax.dot_general(a, b, (((1,), (1,)), ((), ())), preferred_element_type=F32)

    def spread_slab(k, _):
        for h in range(4):
            n = 4 * k + h
            whi, wlo = y_tables(n, WY)
            wtab[0, n] = whi
            wtab[1, n] = wlo
            d = planes - row(ZB, n)
            w = jnp.zeros((16, SLOTS), F32)
            dw = w
            for b in range(ORDER):
                hit = d == b
                w = jnp.where(hit, row(WZ + b, n), w)
                dw = jnp.where(hit, row(DWZ + b, n), dw)
            wzd[n] = w
            dwzd[n] = dw
            hi, lo = split(jnp.concatenate([row(QX + i, n) * w for i in range(4)], axis=0))
            m = nt(hi, whi) + nt(lo, whi) + nt(hi, wlo)
            cur = m[:, :128]
            if h:
                cur = cur + halo[...]
            halo[:, 0:16] = m[:, 128:144]
            lanes = slice(h * 128, (h + 1) * 128)
            u[core, k, :, :, lanes] = cur[:32].reshape(2, 16, 128)
            u[2, k, :, :, lanes] = cur[32:].reshape(2, 16, 128)
        u[core, k, :, :, 0:128] += halo[0:32].reshape(2, 16, 128)
        u[2, k, :, :, 0:128] += halo[32:64].reshape(2, 16, 128)
        remote(u.at[2, k], u.at[core, k], grid_sems, k, sibling).start()
        return 0

    lax.fori_loop(0, SLABS, spread_slab, 0)

    def grid_landed(k, _):
        remote(u.at[2, k], u.at[1 - core, k], grid_sems, k, sibling).wait()
        return 0

    lax.fori_loop(0, SLABS, grid_landed, 0)

    def fwd_y(i, _):
        def planes_of(c, m):
            lanes = slice(m * 128, (m + 1) * 128)
            tiles = []
            for t in range(8):
                below = lax.rem(4 * i + (t - 1) // 2 + SLABS, SLABS)
                tiles.append(u[t % 2, 4 * i + t // 2, c, 0:8, lanes]
                             + u[1 - t % 2, below, c, 8:16, lanes])
            return jnp.concatenate(tiles, axis=0)

        xr = [planes_of(0, m) for m in range(4)]
        xi = [planes_of(1, m) for m in range(4)]
        ar, ai = radix4(xr, xi, -1)
        rows = pl.ds(pl.multiple_of(i * 64, 64), 64)
        for r in range(4):
            if r:
                c, s = twy[0, r:r + 1, :], twy[1, r:r + 1, :]
                ar[r], ai[r] = ar[r] * c + ai[r] * s, ai[r] * c - ar[r] * s
            hi, lo = split(jnp.concatenate([ar[r], ai[r]], axis=1))
            spec[rows, r * 256:(r + 1) * 256] = (
                mm(hi, mats[0, 0]) + mm(lo, mats[0, 0]) + mm(hi, mats[0, 1]))
        return 0

    lax.fori_loop(0, N // 64, fwd_y, 0)

    def left_mm(which, v):
        hi, lo = split(v)
        return mm(mats[which, 0], hi) + mm(mats[which, 1], hi) + mm(mats[which, 0], lo)

    for rp in range(2):
        first = rp * 512

        def lanes_of(part):
            return [slice(first + rr * 256 + part * 128, first + rr * 256 + part * 128 + 128)
                    for rr in range(2)]

        def grab(m, part):
            return jnp.concatenate(
                [spec[m * 128:(m + 1) * 128, l] for l in lanes_of(part)], axis=1)

        ar, ai = radix4([grab(m, 0) for m in range(4)], [grab(m, 1) for m in range(4)], -1)
        for s_ in range(4):
            cc = jnp.concatenate([twz[0, s_]] * 2, axis=1)
            ss = jnp.concatenate([twz[1, s_]] * 2, axis=1)
            if s_:
                ar[s_], ai[s_] = ar[s_] * cc + ai[s_] * ss, ai[s_] * cc - ar[s_] * ss
            f = left_mm(2, jnp.concatenate([ar[s_], ai[s_]], axis=0))
            w = filt[s_ * 128:(s_ + 1) * 128, rp * 256:(rp + 1) * 256]
            f = left_mm(3, f * jnp.concatenate([w, w], axis=0))
            ur, ui = f[:128], f[128:]
            if s_:
                ur, ui = ur * cc - ui * ss, ui * cc + ur * ss
            ar[s_], ai[s_] = ur, ui
        br, bi = radix4(ar, ai, 1)
        for m in range(4):
            for p, v in ((0, br[m]), (1, bi[m])):
                for rr, l in enumerate(lanes_of(p)):
                    spec[m * 128:(m + 1) * 128, l] = v[:, rr * 128:(rr + 1) * 128]

    def pot_copy(i):
        rows = pl.ds(i * 8, 8)
        return remote(hown.at[rows], hsib.at[rows], pot_sems, i, sibling)

    def inv_y(i, _):
        rows = pl.ds(pl.multiple_of(i * 64, 64), 64)
        ar, ai = [], []
        for r in range(4):
            hi, lo = split(spec[rows, r * 256:(r + 1) * 256])
            v = mm(hi, mats[1, 0]) + mm(lo, mats[1, 0]) + mm(hi, mats[1, 1])
            ur, ui = v[:, :128], v[:, 128:]
            if r:
                c, s = twy[0, r:r + 1, :], twy[1, r:r + 1, :]
                ur, ui = ur * c - ui * s, ui * c + ur * s
            ar.append(ur)
            ai.append(ui)
        br, bi = radix4(ar, ai, 1)
        for m in range(4):
            lanes = slice(m * 128, (m + 1) * 128)
            hown[pl.ds(8 * i, 8), 0, :, lanes] = br[m].reshape(8, 8, 128)
            hown[pl.ds(8 * i, 8), 1, :, lanes] = bi[m].reshape(8, 8, 128)
        pot_copy(i).start()
        return 0

    lax.fori_loop(0, 8, inv_y, 0)

    def gather_slab(k, _):
        g = 2 * k + core
        nxt = lax.rem(g + 1, 64)
        for j, ref in enumerate((hown, hsib)):
            for c in range(2):
                hi, lo = split(jnp.concatenate([ref[g, c], ref[nxt, c]], axis=0))
                rows = slice(32 * j + 16 * c, 32 * j + 16 * c + 16)
                for dst, v in ((hs_hi, hi), (hs_lo, lo)):
                    dst[rows, 0:N] = v
                    dst[rows, N:N + 16] = v[:, 0:16]
        for h in range(4):
            n = 4 * k + h
            lanes = slice(h * 128, h * 128 + 144)
            hi, lo = hs_hi[:, lanes], hs_lo[:, lanes]

            def field(whi, wlo):
                return mm(hi, whi) + mm(lo, whi) + mm(hi, wlo)

            a = field(wtab[0, n], wtab[1, n])
            s = field(*y_tables(n, DWY))

            def mix(v, first):
                tot = None
                for i in range(4):
                    term = row(first + i, n) * v[16 * i:16 * i + 16]
                    tot = term if tot is None else tot + term
                return tot

            w, dw = wzd[n], dwzd[n]
            fz = jnp.sum(dw * mix(a, QX), axis=0, keepdims=True)
            fy = jnp.sum(w * mix(s, QX), axis=0, keepdims=True)
            fx = jnp.sum(w * mix(a, P2), axis=0, keepdims=True)
            xk, zk = k // 8, lax.rem(k, 8)
            for d, f in enumerate((fz, fy, fx)):
                for half in range(2):
                    part[xk, zk, h, 2 * d + half:2 * d + half + 1, :] = -f[:, half * 128:(half + 1) * 128]
            part[xk, zk, h, 6:8, :] = jnp.zeros((2, 128), F32)
        return 0

    pot_copy(0).wait()

    def gather_chunk(i, _):
        @pl.when(i < 7)
        def _():
            pot_copy(i + 1).wait()

        lax.fori_loop(0, 4, lambda kk, _: gather_slab(4 * i + kk, 0), 0)
        return 0

    lax.fori_loop(0, 8, gather_chunk, 0)
    total = scatter_forces(part, r1a, r1b, s1a, s1b, r2, s2, r3, rs_sems)
    for d in range(3):
        out[d:d + 1, 0:128] = total[2 * d:2 * d + 1, :]
        out[d:d + 1, 128:256] = total[2 * d + 1:2 * d + 2, :]


def local(charges, grid_base, fraction, counts, influence):
    mats, twy, twz = tables()
    vm = pl.BlockSpec(memory_space=pltpu.VMEM)
    sm = pl.BlockSpec(memory_space=pltpu.SMEM)
    hbm = pl.BlockSpec(memory_space=pl.ANY)
    tile = (8, 128)

    def f32(*shape):
        return pltpu.VMEM(shape, F32)

    return pl.pallas_call(
        main_kernel,
        out_shape=jax.ShapeDtypeStruct((3, SLOTS), F32),
        in_specs=[sm, vm, vm, vm, hbm, hbm, hbm, vm, hbm],
        out_specs=vm,
        scratch_shapes=[
            f32(4 * N, 128),
            pltpu.VMEM((N, N), BF16),
            pltpu.VMEM((4, 2, 256, 256), BF16),
            f32(2, 4, 128, 128),
            f32(4, 8, 4, *tile),
            f32(4, 8, 4, *tile),
            f32(2, 2, 8, SLOTS),
            f32(ROWS, BLOCKS, SLOTS),
            f32(BLOCKS, 16, SLOTS),
            f32(BLOCKS, 16, SLOTS),
            pltpu.VMEM((2, BLOCKS, 144, SLOTS), BF16),
            f32(64, 128),
            f32(3, SLABS, 2, 16, N),
            f32(N, 2 * N),
            f32(N, N),
            f32(64, 2, 8, N),
            f32(64, 2, 8, N),
            pltpu.VMEM((64, N + 128), BF16),
            pltpu.VMEM((64, N + 128), BF16),
            f32(4, 8, 4, *tile),
            f32(4, 4, 4, *tile),
            f32(4, 4, 4, *tile),
            f32(4, 4, *tile),
            f32(4, 4, *tile),
            f32(2, 4, 4, *tile),
            f32(8, *tile),
            f32(8, *tile),
            pltpu.SemaphoreType.DMA((4,)),
            pltpu.SemaphoreType.DMA((2, 32)),
            pltpu.SemaphoreType.DMA((2, SLABS)),
            pltpu.SemaphoreType.DMA((2, 8)),
            pltpu.SemaphoreType.DMA((2, 24)),
        ],
        compiler_params=pltpu.CompilerParams(
            collective_id=0, has_side_effects=True, vmem_limit_bytes=60 * 1024 * 1024),
        cost_estimate=pl.CostEstimate(flops=40_000_000_000, bytes_accessed=4_000_000, transcendentals=0),
    )(counts, charges.reshape(2, 128), grid_base, fraction, influence.reshape(4 * N, 128),
      jnp.asarray(reorder()), jnp.asarray(mats), jnp.asarray(twy), jnp.asarray(twz))


def solution(mesh):
    placed = (
        P(("gz", "gy")),
        P(None, ("gz", "gy")),
        P(None, ("gz", "gy")),
        P("gz", "gy"),
        P(None, ("gy", "gz"), None),
    )
    return jax.shard_map(
        local, mesh=mesh, in_specs=placed, out_specs=P(None, ("gz", "gy")), check_vma=False
    )
```

time: 470 us -> 83 us (0.18); the launches traced: 464 us -> 82.8 us
  waiting for transfers between devices: 157 us -> 0 us
  matrix products: 127 us -> 0 us
  Pallas kernels: 0 us -> 80.9 us
  local copies, waits for them, and re-layouts: 70.3 us -> 1.28 us
  blocking collectives: 48 us -> 0 us
  starting transfers between devices: 32.5 us -> 0 us
  other arithmetic: 27.6 us -> 0 us
    all_to_all x3 -> x0, waiting for transfers between devices: 128 us -> none  [the longest x1 51.2 us: local(): lax.all_to_all(spectrum, 'gz', split_axis=1, concat_axis=2, tiled=True)]
    dot_general x23 -> x0, matrix products: 127 us -> none  [einsum_high(): jnp.einsum(form, left_arr, right_arr, precision=lax.Precision.HIGHEST)]
    pallas_call x0 -> x1, Pallas kernels: none -> 80.9 us  [local(): pl.pallas_call(main_kernel, out_shape=jax.ShapeDtypeStruct((3, SLOTS), F3...]
    all_to_all x1 -> x0, blocking collectives: 48 us -> none  [local(): lax.all_to_all(spectrum, 'gy', split_axis=2, concat_axis=3, tiled=True)]
    ppermute x2 -> x0, waiting for transfers between devices: 29 us -> none  [from_behind(): return lax.ppermute(block, axis, route)]
    all_to_all x3 -> x0, starting transfers between devices: 27.8 us -> none  [the longest x1 18.4 us: local(): lax.all_to_all(spectrum, 'gz', split_axis=2, concat_axis=1, tiled=True)]
    slice x12 -> x0, local copies, waits for them, and re-layouts: 18.4 us -> none  [the longest x2 4.38 us: local(): moved = from_behind(spread[planes:], 'gz', 1)]
    all_to_all x6 -> x0, local copies, waits for them, and re-layouts: 14.9 us -> none  [the longest x1 8.58 us: local(): lax.all_to_all(spectrum, 'gy', split_axis=2, concat_axis=3, tiled=True)]
  transfers between devices with their start and end apart: 5 -> 0, of which waited for: 5 -> 0; matrix products, arithmetic and copies ran while one was open for 1% -> 0% of each run, Pallas kernels for 0% -> 0%
where the time goes in v2:
time: 83 us; the launch traced here: 82.8 us
  Pallas kernels  80.9 us (97%)
  local copies, waits for them, and re-layouts  1.28 us (2%)
    pallas_call x1, Pallas kernels, local(): pl.pallas_call(main_kernel, out_shape=jax.ShapeDtypeStruct((3, SLOTS), F3...  80.9 us

profile of v2, /device:TPU:1, one launch (start us, length us, event | category | flops | bytes accessed | tf_op | source)
XLA Modules:
  0.0 82.8 jit_solution(18437071857121437846)
XLA Ops:
  0.7 80.9 %shard_map.91 = f32[3,256]{1,0:T(4,128)} custom-call(s32[1,1]{1,0:T(1,128)S(6)} %copy.11.counts, f32[2,128]{1,0:T(2,128)} %bitcast.3, s32[3,256]{1,0:T(4,128)} %base.1, f32[3,256]{1,0:T(4,128)} %frac.1, f32[2048,128]{1,0:T(8,128)} %bitcast.2, bf16[512,512]{1,0:T(8,128)(2,1)} %constant.8.clone.perm_hbm, bf16[4,2,256,256]{3,2,1,0:T(8,128)(2,1)} %constant.9.clone.mats_hbm, ...), custom_call_target="tpu_custom_call" | custom-call | flops 40000000000 | bytes 4000000 | tf_op jit(solution)/shard_map/pallas_call | solution.py:524
  81.5 1.3 %copy.12 = f32[3,256]{1,0:T(4,128)} copy(f32[3,256]{1,0:T(4,128)} %shard_map.91) | data formatting | bytes 6144

commit v3 on v2

--- a/solution.py
+++ b/solution.py
@@ -76,6 +76,16 @@
     return hi, (x - hi.astype(F32)).astype(BF16)
 
 
+def stack(x):
+    hi = x.astype(BF16)
+    return jnp.concatenate([hi, (x - hi.astype(F32)).astype(BF16)], axis=0)
+
+
+def halves_sum(x):
+    rows = x.shape[0] // 2
+    return x[:rows] + x[rows:]
+
+
 def mm(a, b):
     return jnp.dot(a, b, preferred_element_type=F32)
 
@@ -136,89 +146,22 @@
         device_id=to, device_id_type=MESH)
 
 
-def gather_atoms(half_a, half_b, sems, meanwhile):
-    x, z, c, y = place()
-    sib = device(x, z, 1 - c, y)
-    flying = []
-
-    def go(ref, to, k):
-        copy = remote(ref, ref, sems, k, to)
+def launch(copies):
+    for copy in copies:
         copy.start()
-        flying.append(copy)
-
-    def landed(ref, k):
-        remote(ref, ref, sems, k, sib).wait_recv()
-
-    for k in range(1, 8):
-        to = device(x, (z + k) % 8, c, y)
-        go(half_a.at[x, z, y], to, k)
-        go(half_b.at[x, z, y], to, 8 + k)
-    meanwhile()
-    for k in range(1, 8):
-        landed(half_a.at[x, (z + 8 - k) % 8, y], k)
-        landed(half_b.at[x, (z + 8 - k) % 8, y], 8 + k)
-    for k in range(1, 4):
-        go(half_a.at[x, :, y], device((x + k) % 4, z, c, y), 16 + k)
-        go(half_b.at[x, :, y], device(x, z, c, (y + k) % 4), 20 + k)
-    for k in range(1, 4):
-        landed(half_a.at[(x + 4 - k) % 4, :, y], 16 + k)
-        landed(half_b.at[x, :, (y + 4 - k) % 4], 20 + k)
-    for k in range(1, 4):
-        go(half_a.at[:, :, y], device(x, z, c, (y + k) % 4), 24 + k)
-        go(half_b.at[x], device((x + k) % 4, z, c, y), 28 + k)
-    for k in range(1, 4):
-        landed(half_a.at[:, :, (y + 4 - k) % 4], 24 + k)
-        landed(half_b.at[(x + 4 - k) % 4], 28 + k)
-    for copy in flying:
+    return copies
+
+
+def settle(copies, arrivals):
+    for copy in arrivals:
+        copy.wait_recv()
+    for copy in copies:
         copy.wait_send()
 
 
-def scatter_forces(full, r1a, r1b, s1a, s1b, r2, s2, r3, sems):
-    x, z, c, y = place()
-    sib = device(x, z, 1 - c, y)
-    flying = []
-
-    def go(src, dst, to, k):
-        copy = remote(src, dst, sems, k, to)
-        copy.start()
-        flying.append(copy)
-
-    def landed(dst, k):
-        remote(dst, dst, sems, k, sib).wait_recv()
-
-    for k in range(1, 4):
-        xk, yk = (x + k) % 4, (y + k) % 4
-        go(full.at[xk, 0:4], r1a.at[k], device(xk, z, c, y), k)
-        go(full.at[:, 4:8, yk], r1b.at[k], device(x, z, c, yk), 4 + k)
-    for k in range(1, 4):
-        landed(r1a.at[k], k)
-        landed(r1b.at[k], 4 + k)
-    s1a[...] = full[x, 0:4] + r1a[1] + r1a[2] + r1a[3]
-    s1b[...] = full[:, 4:8, y] + r1b[1] + r1b[2] + r1b[3]
-    for k in range(1, 4):
-        xk, yk = (x + k) % 4, (y + k) % 4
-        go(s1a.at[:, yk], r2.at[0, k], device(x, z, c, yk), 8 + k)
-        go(s1b.at[xk], r2.at[1, k], device(xk, z, c, y), 12 + k)
-    for k in range(1, 4):
-        landed(r2.at[0, k], 8 + k)
-        landed(r2.at[1, k], 12 + k)
-    s2[0:4] = s1a[:, y] + r2[0, 1] + r2[0, 2] + r2[0, 3]
-    s2[4:8] = s1b[x] + r2[1, 1] + r2[1, 2] + r2[1, 3]
-    for k in range(1, 8):
-        zk = (z + k) % 8
-        go(s2.at[zk], r3.at[k], device(x, zk, c, y), 16 + k)
-    total = s2[z]
-    for k in range(1, 8):
-        landed(r3.at[k], 16 + k)
-        total = total + r3[k]
-    for copy in flying:
-        copy.wait_send()
-    return total
-
-
 def main_kernel(counts, charges, base, frac, infl_hbm, perm_hbm, mats_hbm, twy, twz_hbm, out,
-                infl, perm, mats, twz, half_a, half_b, coefs, prep, wzd, dwzd, wtab, halo, u, spec,
-                filt, hown, hsib, hs_hi, hs_lo, part, r1a, r1b, s1a, s1b, r2, s2, r3,
+                infl, perm, mats, twz, zbuf, at_a, at_b, coefs, prep, wzd, dwzd, wtab, u, spec,
+                filt, hown, hsib, part_a, part_b, r1, s1a, s1b, r2, s2, r3,
                 local_sems, ag_sems, grid_sems, pot_sems, rs_sems):
     x, z, core, y = place()
     sibling = device(x, z, 1 - core, y)
@@ -235,40 +178,73 @@
         load.start()
     meet()
 
-    for half, ref in enumerate((half_a, half_b)):
+    for half in range(2):
         lanes = slice(half * 128, half * 128 + 128)
         slots = lax.broadcasted_iota(jnp.int32, (1, 128), 1) + half * 128
         q = jnp.where(slots < counts[0, 0], charges[half:half + 1, :], 0.0)
-        ref[x, z, y] = jnp.concatenate(
+        zbuf[z, half] = jnp.concatenate(
             [q, (base[0:1, lanes] - gz * CZ).astype(F32), (base[1:2, lanes] - y * CY).astype(F32),
              base[2:3, lanes].astype(F32), frac[:, lanes], jnp.zeros((1, 128), F32)], axis=0)
 
-    def meanwhile():
-        c_rows = lax.broadcasted_iota(jnp.int32, (8, SLOTS), 0)
-        for j in range(2):
-            cs, sn = turn(c_rows * kxs[j])
-            coefs[j, 0] = cs
-            coefs[j, 1] = sn
-        for load in loads:
-            load.wait()
-        scale = jnp.where(kx == 0, 1.0, 2.0) / float(N) ** 3
-        for s_ in range(4):
-            rows = jnp.concatenate(
-                [infl[pl.ds(4 * s_ + t, 128, stride=16), :] for t in range(4)], axis=1)
-            hi, lo = split(rows * scale)
-            filt[s_ * 128:(s_ + 1) * 128, :] = mm(hi, perm[...]) + mm(lo, perm[...])
-        halo[...] = jnp.zeros_like(halo)
-
-    gather_atoms(half_a, half_b, ag_sems, meanwhile)
-    flat = [half.reshape(BLOCKS * 8, 128) for half in (half_a, half_b)]
-
-    def prepare(i, _):
+    def sender(src, dst, to, k):
+        return remote(src, dst, ag_sems, k, to)
+
+    first = launch([sender(zbuf.at[z], zbuf.at[z], device(x, (z + k) % 8, core, y), k)
+                    for k in range(1, 8)])
+    c_rows = lax.broadcasted_iota(jnp.int32, (8, SLOTS), 0)
+    for j in range(2):
+        cs, sn = turn(c_rows * kxs[j])
+        coefs[j, 0] = cs
+        coefs[j, 1] = sn
+    u[core] = jnp.zeros(u.shape[1:], F32)
+    u[2] = jnp.zeros(u.shape[1:], F32)
+    settle(first, [sender(zbuf.at[(z + 8 - k) % 8], zbuf.at[(z + 8 - k) % 8], sibling, k)
+                   for k in range(1, 8)])
+    for zz in range(4):
+        at_a[y, 4 * x + zz] = zbuf[zz]
+        at_b[x, zz, y] = zbuf[4 + zz]
+
+    def row_a(xx):
+        return at_a.at[y, pl.ds(4 * xx, 4)]
+
+    def row_b(yy):
+        return at_b.at[x, :, yy]
+
+    second = launch(
+        [sender(row_a(x), row_a(x), device((x + k) % 4, z, core, y), 8 + k) for k in range(1, 4)]
+        + [sender(row_b(y), row_b(y), device(x, z, core, (y + k) % 4), 12 + k) for k in range(1, 4)])
+    for load in loads:
+        load.wait()
+    scale = jnp.where(kx == 0, 1.0, 2.0) / float(N) ** 3
+    for s_ in range(4):
+        rows = jnp.concatenate(
+            [infl[pl.ds(4 * s_ + t, 128, stride=16), :] for t in range(4)], axis=1)
+        filt[s_ * 128:(s_ + 1) * 128, :] = halves_sum(mm(stack(rows * scale), perm[...]))
+    settle(second,
+           [sender(row_a((x + 4 - k) % 4), row_a((x + 4 - k) % 4), sibling, 8 + k) for k in range(1, 4)]
+           + [sender(row_b((y + 4 - k) % 4), row_b((y + 4 - k) % 4), sibling, 12 + k) for k in range(1, 4)])
+
+    def third(k):
+        return [sender(at_a.at[y], at_a.at[y], device(x, z, core, (y + k) % 4), 16 + k),
+                sender(at_b.at[x], at_b.at[x], device((x + k) % 4, z, core, y), 20 + k)]
+
+    def third_from(k):
+        ya, xb = (y + 4 - k) % 4, (x + 4 - k) % 4
+        return [sender(at_a.at[ya], at_a.at[ya], sibling, 16 + k),
+                sender(at_b.at[xb], at_b.at[xb], sibling, 20 + k)]
+
+    launch(third(1) + third(3))
+
+    flat_a = at_a.reshape(64 * 16, 128)
+    flat_b = at_b.reshape(64 * 16, 128)
+
+    def prepare(flat, i, offset):
         def comp(j):
             return jnp.concatenate(
-                [half[pl.ds(64 * i + j, 8, stride=8), :] for half in flat], axis=1)
+                [flat[pl.ds(128 * i + 8 * half + j, 8, stride=16), :] for half in range(2)], axis=1)
 
         def put(k, v):
-            prep[k, pl.ds(pl.multiple_of(8 * i, 8), 8), :] = v
+            prep[k, pl.ds(pl.multiple_of(8 * i + offset, 8), 8), :] = v
 
         q = comp(0)
         wz, dwz = spline_six(comp(4))
@@ -302,9 +278,6 @@
         put(ZB, comp(1))
         put(YL, (yb & 15).astype(F32))
         put(YT, (yb >> 4).astype(F32))
-        return 0
-
-    lax.fori_loop(0, BLOCKS // 8, prepare, 0)
 
     def row(k, n):
         return prep[k, pl.ds(n, 1), :]
@@ -333,9 +306,12 @@
     def nt(a, b):
         return lax.dot_general(a, b, (((1,), (1,)), ((), ())), preferred_element_type=F32)
 
-    def spread_slab(k, _):
-        for h in range(4):
-            n = 4 * k + h
+    def spread_four(xx, first_z, h, block):
+        here = pl.ds(pl.multiple_of(h * 128, 128), 128)
+        after = pl.ds(pl.multiple_of(lax.rem(h + 1, 4) * 128, 128), 16)
+        for zz in range(4):
+            n = block(zz)
+            k = 8 * xx + first_z + zz
             whi, wlo = y_tables(n, WY)
             wtab[0, n] = whi
             wtab[1, n] = wlo
@@ -348,27 +324,73 @@
                 dw = jnp.where(hit, row(DWZ + b, n), dw)
             wzd[n] = w
             dwzd[n] = dw
-            hi, lo = split(jnp.concatenate([row(QX + i, n) * w for i in range(4)], axis=0))
-            m = nt(hi, whi) + nt(lo, whi) + nt(hi, wlo)
-            cur = m[:, :128]
-            if h:
-                cur = cur + halo[...]
-            halo[:, 0:16] = m[:, 128:144]
-            lanes = slice(h * 128, (h + 1) * 128)
-            u[core, k, :, :, lanes] = cur[:32].reshape(2, 16, 128)
-            u[2, k, :, :, lanes] = cur[32:].reshape(2, 16, 128)
-        u[core, k, :, :, 0:128] += halo[0:32].reshape(2, 16, 128)
-        u[2, k, :, :, 0:128] += halo[32:64].reshape(2, 16, 128)
-        remote(u.at[2, k], u.at[core, k], grid_sems, k, sibling).start()
+            both = stack(jnp.concatenate([row(QX + i, n) * w for i in range(4)], axis=0))
+            m = halves_sum(nt(both, whi)) + nt(both[:64], wlo)
+            for j, plane in ((0, core), (1, 2)):
+                v = m[32 * j:32 * j + 32]
+                u[plane, k, :, :, here] += v[:, :128].reshape(2, 16, 128)
+                u[plane, k, :, :, after] += v[:, 128:144].reshape(2, 16, 16)
+
+    def swap(k):
+        return remote(u.at[2, k], u.at[core, k], grid_sems, k, sibling)
+
+    def spread_phase(ya, xb):
+        def part_of_a(xx, _):
+            spread_four(xx, 0, ya, lambda zz: 16 * ya + 4 * xx + zz)
+            return 0
+
+        def part_of_b(h, _):
+            spread_four(xb, 4, h, lambda zz: 64 + 16 * xb + 4 * zz + h)
+            return 0
+
+        def prepare_two(i, _):
+            prepare(flat_a, 2 * ya + i, 0)
+            prepare(flat_b, 2 * xb + i, 64)
+            return 0
+
+        lax.fori_loop(0, 2, prepare_two, 0)
+        lax.fori_loop(0, 4, part_of_b, 0)
+        for zz in range(4):
+            swap(8 * xb + 4 + zz).start()
+        lax.fori_loop(0, 4, part_of_a, 0)
+
+    def spread_step(p, _):
+        @pl.when(p == 1)
+        def _():
+            launch(third(2))
+            settle([], third_from(1))
+
+        @pl.when(p == 2)
+        def _():
+            settle([], third_from(3))
+
+        @pl.when(p == 3)
+        def _():
+            settle([], third_from(2))
+
+        off = lax.rem(3 * p, 4) * (1 - p // 2) + (p // 2) * (p - 1)
+        spread_phase(lax.rem(y + off, 4), lax.rem(x + off, 4))
         return 0
 
-    lax.fori_loop(0, SLABS, spread_slab, 0)
+    lax.fori_loop(0, 4, spread_step, 0)
+    for xx in range(4):
+        for zz in range(4):
+            swap(8 * xx + zz).start()
+    for k in range(1, 4):
+        for copy in third(k):
+            copy.wait_send()
 
     def grid_landed(k, _):
         remote(u.at[2, k], u.at[1 - core, k], grid_sems, k, sibling).wait()
         return 0
 
     lax.fori_loop(0, SLABS, grid_landed, 0)
+
+    def right_mm(v, which):
+        rows = v.shape[0]
+        both = stack(v)
+        t = mm(both, mats[which, 0])
+        return t[:rows] + t[rows:] + mm(both[:rows], mats[which, 1])
 
     def fwd_y(i, _):
         def planes_of(c, m):
@@ -388,16 +410,15 @@
             if r:
                 c, s = twy[0, r:r + 1, :], twy[1, r:r + 1, :]
                 ar[r], ai[r] = ar[r] * c + ai[r] * s, ai[r] * c - ar[r] * s
-            hi, lo = split(jnp.concatenate([ar[r], ai[r]], axis=1))
-            spec[rows, r * 256:(r + 1) * 256] = (
-                mm(hi, mats[0, 0]) + mm(lo, mats[0, 0]) + mm(hi, mats[0, 1]))
+            spec[rows, r * 256:(r + 1) * 256] = right_mm(jnp.concatenate([ar[r], ai[r]], axis=1), 0)
         return 0
 
     lax.fori_loop(0, N // 64, fwd_y, 0)
 
     def left_mm(which, v):
         hi, lo = split(v)
-        return mm(mats[which, 0], hi) + mm(mats[which, 1], hi) + mm(mats[which, 0], lo)
+        t = mm(mats[which].reshape(512, 256), hi)
+        return t[:256] + t[256:] + mm(mats[which, 0], lo)
 
     for rp in range(2):
         first = rp * 512
@@ -437,8 +458,7 @@
         rows = pl.ds(pl.multiple_of(i * 64, 64), 64)
         ar, ai = [], []
         for r in range(4):
-            hi, lo = split(spec[rows, r * 256:(r + 1) * 256])
-            v = mm(hi, mats[1, 0]) + mm(lo, mats[1, 0]) + mm(hi, mats[1, 1])
+            v = right_mm(spec[rows, r * 256:(r + 1) * 256], 1)
             ur, ui = v[:, :128], v[:, 128:]
             if r:
                 c, s = twy[0, r:r + 1, :], twy[1, r:r + 1, :]
@@ -455,23 +475,23 @@
 
     lax.fori_loop(0, 8, inv_y, 0)
 
-    def gather_slab(k, _):
-        g = 2 * k + core
-        nxt = lax.rem(g + 1, 64)
-        for j, ref in enumerate((hown, hsib)):
-            for c in range(2):
-                hi, lo = split(jnp.concatenate([ref[g, c], ref[nxt, c]], axis=0))
-                rows = slice(32 * j + 16 * c, 32 * j + 16 * c + 16)
-                for dst, v in ((hs_hi, hi), (hs_lo, lo)):
-                    dst[rows, 0:N] = v
-                    dst[rows, N:N + 16] = v[:, 0:16]
-        for h in range(4):
-            n = 4 * k + h
-            lanes = slice(h * 128, h * 128 + 144)
-            hi, lo = hs_hi[:, lanes], hs_lo[:, lanes]
+    def gather_four(xx, first_z, h, block, put):
+        here = pl.ds(pl.multiple_of(h * 128, 128), 128)
+        after = pl.ds(pl.multiple_of(lax.rem(h + 1, 4) * 128, 128), 128)
+        for zz in range(4):
+            n = block(zz)
+            g = 2 * (8 * xx + first_z + zz) + core
+            nxt = lax.rem(g + 1, 64)
+            fields = [
+                jnp.concatenate(
+                    [jnp.concatenate([ref[t, c, :, here], ref[t, c, :, after]], axis=1)
+                     for t in (g, nxt)], axis=0)
+                for ref in (hown, hsib) for c in range(2)
+            ]
+            both = stack(jnp.concatenate(fields, axis=0))[:, :144]
 
             def field(whi, wlo):
-                return mm(hi, whi) + mm(lo, whi) + mm(hi, wlo)
+                return halves_sum(mm(both, whi)) + mm(both[:64], wlo)
 
             a = field(wtab[0, n], wtab[1, n])
             s = field(*y_tables(n, DWY))
@@ -487,28 +507,74 @@
             fz = jnp.sum(dw * mix(a, QX), axis=0, keepdims=True)
             fy = jnp.sum(w * mix(s, QX), axis=0, keepdims=True)
             fx = jnp.sum(w * mix(a, P2), axis=0, keepdims=True)
-            xk, zk = k // 8, lax.rem(k, 8)
-            for d, f in enumerate((fz, fy, fx)):
-                for half in range(2):
-                    part[xk, zk, h, 2 * d + half:2 * d + half + 1, :] = -f[:, half * 128:(half + 1) * 128]
-            part[xk, zk, h, 6:8, :] = jnp.zeros((2, 128), F32)
+            put(zz, jnp.concatenate(
+                [-f[:, half * 128:(half + 1) * 128] for f in (fz, fy, fx) for half in range(2)]
+                + [jnp.zeros((2, 128), F32)], axis=0))
+
+    def shares(off):
+        return [remote(part_a.at[(y + off) % 4], r1.at[0, off], rs_sems, off,
+                       device(x, z, core, (y + off) % 4)),
+                remote(part_b.at[(x + off) % 4], r1.at[1, off], rs_sems, 4 + off,
+                       device((x + off) % 4, z, core, y))]
+
+    for i in range(8):
+        pot_copy(i).wait()
+
+    def gather_step(p, _):
+        off = (p == 0) * 2 + (p == 1) * 1 + (p == 2) * 3
+        ya, xb = lax.rem(y + off, 4), lax.rem(x + off, 4)
+
+        def part_of_a(xx, _):
+            def put(zz, v):
+                part_a[ya, xx, zz] = v
+
+            gather_four(xx, 0, ya, lambda zz: 16 * ya + 4 * xx + zz, put)
+            return 0
+
+        def part_of_b(h, _):
+            def put(zz, v):
+                part_b[xb, zz, h] = v
+
+            gather_four(xb, 4, h, lambda zz: 64 + 16 * xb + 4 * zz + h, put)
+            return 0
+
+        lax.fori_loop(0, 4, part_of_b, 0)
+        lax.fori_loop(0, 4, part_of_a, 0)
+        for step, away in enumerate((2, 1, 3)):
+            @pl.when(p == step)
+            def _():
+                launch(shares(away))
+
         return 0
 
-    pot_copy(0).wait()
-
-    def gather_chunk(i, _):
-        @pl.when(i < 7)
-        def _():
-            pot_copy(i + 1).wait()
-
-        lax.fori_loop(0, 4, lambda kk, _: gather_slab(4 * i + kk, 0), 0)
-        return 0
-
-    lax.fori_loop(0, 8, gather_chunk, 0)
-    total = scatter_forces(part, r1a, r1b, s1a, s1b, r2, s2, r3, rs_sems)
+    lax.fori_loop(0, 4, gather_step, 0)
+    for k in range(1, 4):
+        settle([], shares(k))
+    s1a[...] = part_a[y] + r1[0, 1] + r1[0, 2] + r1[0, 3]
+    s1b[...] = part_b[x] + r1[1, 1] + r1[1, 2] + r1[1, 3]
+
+    def passed(src, dst, to, k):
+        return remote(src, dst, rs_sems, k, to)
+
+    later = launch(
+        [passed(s1a.at[(x + k) % 4], r2.at[0, k], device((x + k) % 4, z, core, y), 8 + k) for k in range(1, 4)]
+        + [passed(s1b.at[:, (y + k) % 4], r2.at[1, k], device(x, z, core, (y + k) % 4), 12 + k) for k in range(1, 4)])
+    settle([], later)
+    s2[0:4] = s1a[x] + r2[0, 1] + r2[0, 2] + r2[0, 3]
+    s2[4:8] = s1b[:, y] + r2[1, 1] + r2[1, 2] + r2[1, 3]
+    last = launch([passed(s2.at[(z + k) % 8], r3.at[k], device(x, (z + k) % 8, core, y), 16 + k)
+                   for k in range(1, 8)])
+    settle([], last)
+    total = s2[z]
+    for k in range(1, 8):
+        total = total + r3[k]
     for d in range(3):
         out[d:d + 1, 0:128] = total[2 * d:2 * d + 1, :]
         out[d:d + 1, 128:256] = total[2 * d + 1:2 * d + 2, :]
+    settle(later + last, [])
+    for k in range(1, 4):
+        for copy in shares(k):
+            copy.wait_send()
 
 
 def local(charges, grid_base, fraction, counts, influence):
@@ -531,24 +597,22 @@
             pltpu.VMEM((N, N), BF16),
             pltpu.VMEM((4, 2, 256, 256), BF16),
             f32(2, 4, 128, 128),
-            f32(4, 8, 4, *tile),
-            f32(4, 8, 4, *tile),
+            f32(8, 2, *tile),
+            f32(4, 16, 2, *tile),
+            f32(4, 4, 4, 2, *tile),
             f32(2, 2, 8, SLOTS),
             f32(ROWS, BLOCKS, SLOTS),
             f32(BLOCKS, 16, SLOTS),
             f32(BLOCKS, 16, SLOTS),
             pltpu.VMEM((2, BLOCKS, 144, SLOTS), BF16),
-            f32(64, 128),
             f32(3, SLABS, 2, 16, N),
             f32(N, 2 * N),
             f32(N, N),
             f32(64, 2, 8, N),
             f32(64, 2, 8, N),
-            pltpu.VMEM((64, N + 128), BF16),
-            pltpu.VMEM((64, N + 128), BF16),
-            f32(4, 8, 4, *tile),
             f32(4, 4, 4, *tile),
             f32(4, 4, 4, *tile),
+            f32(2, 4, 4, 4, *tile),
             f32(4, 4, *tile),
             f32(4, 4, *tile),
             f32(2, 4, 4, *tile),

time: 83 us -> 73.4 us (0.88)
  Pallas kernels: 80.9 us -> 71 us
    pallas_call x1, Pallas kernels: 80.9 us -> 71 us  [local(): pl.pallas_call(main_kernel, out_shape=jax.ShapeDtypeStruct((3, SLOTS), F3...]
where the time goes in v3:
time: 73.4 us; the launch traced here: 72.9 us
  Pallas kernels  71 us (97%)
  local copies, waits for them, and re-layouts  1.28 us (2%)
    pallas_call x1, Pallas kernels, local(): pl.pallas_call(main_kernel, out_shape=jax.ShapeDtypeStruct((3, SLOTS), F3...  71 us

profile of v3, /device:TPU:1, one launch (start us, length us, event | category | flops | bytes accessed | tf_op | source)
XLA Modules:
  0.0 72.9 jit_solution(5229660602492968004)
XLA Ops:
  0.7 71.0 %shard_map.91 = f32[3,256]{1,0:T(4,128)} custom-call(s32[1,1]{1,0:T(1,128)S(6)} %copy.11.counts, f32[2,128]{1,0:T(2,128)} %bitcast.3, s32[3,256]{1,0:T(4,128)} %base.1, f32[3,256]{1,0:T(4,128)} %frac.1, f32[2048,128]{1,0:T(8,128)} %bitcast.2, bf16[512,512]{1,0:T(8,128)(2,1)} %constant.8.clone.perm_hbm, bf16[4,2,256,256]{3,2,1,0:T(8,128)(2,1)} %constant.9.clone.mats_hbm, ...), custom_call_target="tpu_custom_call" | custom-call | flops 40000000000 | bytes 4000000 | tf_op jit(solution)/shard_map/pallas_call | solution.py:590
  71.7 1.3 %copy.12 = f32[3,256]{1,0:T(4,128)} copy(f32[3,256]{1,0:T(4,128)} %shard_map.91) | data formatting | bytes 6144

commit v4 on v3

--- a/solution.py
+++ b/solution.py
@@ -133,11 +133,14 @@
         yield device(x, (z + k) % 8, c, y)
 
 
-def meet():
-    barrier = pltpu.get_barrier_semaphore()
+def greet():
     for peer in peers():
-        pl.semaphore_signal(barrier, inc=1, device_id=peer, device_id_type=MESH)
-    pl.semaphore_wait(barrier, 14)
+        pl.semaphore_signal(
+            pltpu.get_barrier_semaphore(), inc=1, device_id=peer, device_id_type=MESH)
+
+
+def met():
+    pl.semaphore_wait(pltpu.get_barrier_semaphore(), 14)
 
 
 def remote(src, dst, sems, k, to):
@@ -161,14 +164,15 @@
 
 def main_kernel(counts, charges, base, frac, infl_hbm, perm_hbm, mats_hbm, twy, twz_hbm, out,
                 infl, perm, mats, twz, zbuf, at_a, at_b, coefs, prep, wzd, dwzd, wtab, u, spec,
-                filt, hown, hsib, part_a, part_b, r1, s1a, s1b, r2, s2, r3,
-                local_sems, ag_sems, grid_sems, pot_sems, rs_sems):
+                filt, hown, hsib, part_a, part_b, r1, s1a, s1b, r2,
+                local_sems, ag_sems, grid_sems, pot_sems, rs_sems, end_sems):
     x, z, core, y = place()
     sibling = device(x, z, 1 - core, y)
     gz = lax.axis_index("gz")
     kx = y * 64 + gz
     kxs = (kx, kx + 1 - 2 * core)
 
+    greet()
     loads = [
         pltpu.make_async_copy(src, dst, local_sems.at[i])
         for i, (src, dst) in enumerate(
@@ -176,7 +180,6 @@
     ]
     for load in loads:
         load.start()
-    meet()
 
     for half in range(2):
         lanes = slice(half * 128, half * 128 + 128)
@@ -189,8 +192,6 @@
     def sender(src, dst, to, k):
         return remote(src, dst, ag_sems, k, to)
 
-    first = launch([sender(zbuf.at[z], zbuf.at[z], device(x, (z + k) % 8, core, y), k)
-                    for k in range(1, 8)])
     c_rows = lax.broadcasted_iota(jnp.int32, (8, SLOTS), 0)
     for j in range(2):
         cs, sn = turn(c_rows * kxs[j])
@@ -198,6 +199,10 @@
         coefs[j, 1] = sn
     u[core] = jnp.zeros(u.shape[1:], F32)
     u[2] = jnp.zeros(u.shape[1:], F32)
+    met()
+
+    first = launch([sender(zbuf.at[z], zbuf.at[z], device(x, (z + k) % 8, core, y), k)
+                    for k in range(1, 8)])
     settle(first, [sender(zbuf.at[(z + 8 - k) % 8], zbuf.at[(z + 8 - k) % 8], sibling, k)
                    for k in range(1, 8)])
     for zz in range(4):
@@ -309,9 +314,9 @@
     def spread_four(xx, first_z, h, block):
         here = pl.ds(pl.multiple_of(h * 128, 128), 128)
         after = pl.ds(pl.multiple_of(lax.rem(h + 1, 4) * 128, 128), 16)
+        sums = []
         for zz in range(4):
             n = block(zz)
-            k = 8 * xx + first_z + zz
             whi, wlo = y_tables(n, WY)
             wtab[0, n] = whi
             wtab[1, n] = wlo
@@ -325,7 +330,9 @@
             wzd[n] = w
             dwzd[n] = dw
             both = stack(jnp.concatenate([row(QX + i, n) * w for i in range(4)], axis=0))
-            m = halves_sum(nt(both, whi)) + nt(both[:64], wlo)
+            sums.append(halves_sum(nt(both, whi)) + nt(both[:64], wlo))
+        for zz, m in enumerate(sums):
+            k = 8 * xx + first_z + zz
             for j, plane in ((0, core), (1, 2)):
                 v = m[32 * j:32 * j + 32]
                 u[plane, k, :, :, here] += v[:, :128].reshape(2, 16, 128)
@@ -348,11 +355,11 @@
             prepare(flat_b, 2 * xb + i, 64)
             return 0
 
-        lax.fori_loop(0, 2, prepare_two, 0)
-        lax.fori_loop(0, 4, part_of_b, 0)
+        lax.fori_loop(0, 2, prepare_two, 0, unroll=True)
+        lax.fori_loop(0, 4, part_of_b, 0, unroll=True)
+        lax.fori_loop(0, 4, part_of_a, 0, unroll=True)
         for zz in range(4):
             swap(8 * xb + 4 + zz).start()
-        lax.fori_loop(0, 4, part_of_a, 0)
 
     def spread_step(p, _):
         @pl.when(p == 1)
@@ -413,7 +420,7 @@
             spec[rows, r * 256:(r + 1) * 256] = right_mm(jnp.concatenate([ar[r], ai[r]], axis=1), 0)
         return 0
 
-    lax.fori_loop(0, N // 64, fwd_y, 0)
+    lax.fori_loop(0, N // 64, fwd_y, 0, unroll=2)
 
     def left_mm(which, v):
         hi, lo = split(v)
@@ -473,7 +480,7 @@
         pot_copy(i).start()
         return 0
 
-    lax.fori_loop(0, 8, inv_y, 0)
+    lax.fori_loop(0, 8, inv_y, 0, unroll=2)
 
     def gather_four(xx, first_z, h, block, put):
         here = pl.ds(pl.multiple_of(h * 128, 128), 128)
@@ -538,8 +545,8 @@
             gather_four(xb, 4, h, lambda zz: 64 + 16 * xb + 4 * zz + h, put)
             return 0
 
-        lax.fori_loop(0, 4, part_of_b, 0)
-        lax.fori_loop(0, 4, part_of_a, 0)
+        lax.fori_loop(0, 4, part_of_b, 0, unroll=True)
+        lax.fori_loop(0, 4, part_of_a, 0, unroll=True)
         for step, away in enumerate((2, 1, 3)):
             @pl.when(p == step)
             def _():
@@ -553,25 +560,44 @@
     s1a[...] = part_a[y] + r1[0, 1] + r1[0, 2] + r1[0, 3]
     s1b[...] = part_b[x] + r1[1, 1] + r1[1, 2] + r1[1, 3]
 
-    def passed(src, dst, to, k):
-        return remote(src, dst, rs_sems, k, to)
-
-    later = launch(
-        [passed(s1a.at[(x + k) % 4], r2.at[0, k], device((x + k) % 4, z, core, y), 8 + k) for k in range(1, 4)]
-        + [passed(s1b.at[:, (y + k) % 4], r2.at[1, k], device(x, z, core, (y + k) % 4), 12 + k) for k in range(1, 4)])
-    settle([], later)
-    s2[0:4] = s1a[x] + r2[0, 1] + r2[0, 2] + r2[0, 3]
-    s2[4:8] = s1b[:, y] + r2[1, 1] + r2[1, 2] + r2[1, 3]
-    last = launch([passed(s2.at[(z + k) % 8], r3.at[k], device(x, (z + k) % 8, core, y), 16 + k)
-                   for k in range(1, 8)])
-    settle([], last)
-    total = s2[z]
-    for k in range(1, 8):
-        total = total + r3[k]
+    def sends(src, lead, to, slot):
+        return pltpu.make_async_remote_copy(
+            src_ref=src, dst_ref=r2.at[slot], send_sem=end_sems.at[0, lead],
+            recv_sem=end_sems.at[1, slot], device_id=to, device_id_type=MESH)
+
+    me_a = 4 * z + x
+    me_b = 4 * z + y
+    outgoing = []
+    for zz in range(4):
+        for k in range(4):
+            outgoing.append((s1a.at[k, zz], device(k, zz, core, y), me_a, (k == x) & (zz == z)))
+            outgoing.append((s1b.at[zz, k], device(x, zz + 4, core, k), me_b, (k == y) & (zz + 4 == z)))
+    for lead, (src, to, slot, mine) in enumerate(outgoing):
+        @pl.when(jnp.logical_not(mine))
+        def _():
+            sends(src, lead, to, slot).start()
+
+        @pl.when(mine)
+        def _():
+            r2[slot] = src[...]
+
+    me = jnp.where(z < 4, me_a, me_b)
+    for slot in range(32):
+        @pl.when(slot != me)
+        def _():
+            sends(r2.at[slot], 0, sibling, slot).wait_recv()
+
+    total = r2[0]
+    for slot in range(1, 32):
+        total = total + r2[slot]
     for d in range(3):
         out[d:d + 1, 0:128] = total[2 * d:2 * d + 1, :]
         out[d:d + 1, 128:256] = total[2 * d + 1:2 * d + 2, :]
-    settle(later + last, [])
+    for lead, (src, to, slot, mine) in enumerate(outgoing):
+        @pl.when(jnp.logical_not(mine))
+        def _():
+            sends(src, lead, to, slot).wait_send()
+
     for k in range(1, 4):
         for copy in shares(k):
             copy.wait_send()
@@ -615,14 +641,13 @@
             f32(2, 4, 4, 4, *tile),
             f32(4, 4, *tile),
             f32(4, 4, *tile),
-            f32(2, 4, 4, *tile),
-            f32(8, *tile),
-            f32(8, *tile),
+            f32(32, *tile),
             pltpu.SemaphoreType.DMA((4,)),
             pltpu.SemaphoreType.DMA((2, 32)),
             pltpu.SemaphoreType.DMA((2, SLABS)),
             pltpu.SemaphoreType.DMA((2, 8)),
-            pltpu.SemaphoreType.DMA((2, 24)),
+            pltpu.SemaphoreType.DMA((2, 8)),
+            pltpu.SemaphoreType.DMA((2, 32)),
         ],
         compiler_params=pltpu.CompilerParams(
             collective_id=0, has_side_effects=True, vmem_limit_bytes=60 * 1024 * 1024),

time: 73.4 us -> 65.9 us (0.90)
  Pallas kernels: 71 us -> 63.8 us
    pallas_call x1, Pallas kernels: 71 us -> 63.8 us  [local(): pl.pallas_call(main_kernel, out_shape=jax.ShapeDtypeStruct((3, SLOTS), F3...]
where the time goes in v4:
time: 65.9 us; the launch traced here: 65.7 us
  Pallas kernels  63.8 us (97%)
  local copies, waits for them, and re-layouts  1.28 us (2%)
  between operations  0.66 us (1%)
    pallas_call x1, Pallas kernels, local(): pl.pallas_call(main_kernel, out_shape=jax.ShapeDtypeStruct((3, SLOTS), F3...  63.8 us

profile of v4, /device:TPU:1, one launch (start us, length us, event | category | flops | bytes accessed | tf_op | source)
XLA Modules:
  0.0 65.7 jit_solution(3680162790377413641)
XLA Ops:
  0.7 63.8 %shard_map.91 = f32[3,256]{1,0:T(4,128)} custom-call(s32[1,1]{1,0:T(1,128)S(6)} %copy.11.counts, f32[2,128]{1,0:T(2,128)} %bitcast.3, s32[3,256]{1,0:T(4,128)} %base.1, f32[3,256]{1,0:T(4,128)} %frac.1, f32[2048,128]{1,0:T(8,128)} %bitcast.2, bf16[512,512]{1,0:T(8,128)(2,1)} %constant.8.clone.perm_hbm, bf16[4,2,256,256]{3,2,1,0:T(8,128)(2,1)} %constant.9.clone.mats_hbm, ...), custom_call_target="tpu_custom_call" | custom-call | flops 40000000000 | bytes 4000000 | tf_op jit(solution)/shard_map/pallas_call | solution.py:616
  64.4 1.3 %copy.12 = f32[3,256]{1,0:T(4,128)} copy(f32[3,256]{1,0:T(4,128)} %shard_map.91) | data formatting | bytes 6144

commit v5 on v4

--- a/solution.py
+++ b/solution.py
@@ -164,7 +164,7 @@
 
 def main_kernel(counts, charges, base, frac, infl_hbm, perm_hbm, mats_hbm, twy, twz_hbm, out,
                 infl, perm, mats, twz, zbuf, at_a, at_b, coefs, prep, wzd, dwzd, wtab, u, spec,
-                filt, hown, hsib, part_a, part_b, r1, s1a, s1b, r2,
+                filt, hown, hsib, part, r1, s1, r2,
                 local_sems, ag_sems, grid_sems, pot_sems, rs_sems, end_sems):
     x, z, core, y = place()
     sibling = device(x, z, 1 - core, y)
@@ -380,18 +380,15 @@
         return 0
 
     lax.fori_loop(0, 4, spread_step, 0)
-    for xx in range(4):
-        for zz in range(4):
+    for zz in (3, 0, 1, 2):
+        for xx in range(4):
             swap(8 * xx + zz).start()
     for k in range(1, 4):
         for copy in third(k):
             copy.wait_send()
 
-    def grid_landed(k, _):
+    def grid_landed(k):
         remote(u.at[2, k], u.at[1 - core, k], grid_sems, k, sibling).wait()
-        return 0
-
-    lax.fori_loop(0, SLABS, grid_landed, 0)
 
     def right_mm(v, which):
         rows = v.shape[0]
@@ -420,7 +417,14 @@
             spec[rows, r * 256:(r + 1) * 256] = right_mm(jnp.concatenate([ar[r], ai[r]], axis=1), 0)
         return 0
 
-    lax.fori_loop(0, N // 64, fwd_y, 0, unroll=2)
+    for xx in range(4):
+        for k in range(3, 8):
+            grid_landed(8 * xx + k)
+    lax.fori_loop(0, 4, lambda xx, _: fwd_y(2 * xx + 1, 0), 0, unroll=2)
+    for xx in range(4):
+        for k in range(3):
+            grid_landed(8 * xx + k)
+    lax.fori_loop(0, 4, lambda xx, _: fwd_y(2 * xx, 0), 0, unroll=2)
 
     def left_mm(which, v):
         hi, lo = split(v)
@@ -480,7 +484,8 @@
         pot_copy(i).start()
         return 0
 
-    lax.fori_loop(0, 8, inv_y, 0, unroll=2)
+    lead = 2 * lax.rem(x + 2, 4) + 1
+    lax.fori_loop(0, 8, lambda i, _: inv_y(lax.rem(lead + i, 8), 0), 0, unroll=2)
 
     def gather_four(xx, first_z, h, block, put):
         here = pl.ds(pl.multiple_of(h * 128, 128), 128)
@@ -518,74 +523,82 @@
                 [-f[:, half * 128:(half + 1) * 128] for f in (fz, fy, fx) for half in range(2)]
                 + [jnp.zeros((2, 128), F32)], axis=0))
 
-    def shares(off):
-        return [remote(part_a.at[(y + off) % 4], r1.at[0, off], rs_sems, off,
-                       device(x, z, core, (y + off) % 4)),
-                remote(part_b.at[(x + off) % 4], r1.at[1, off], rs_sems, 4 + off,
-                       device((x + off) % 4, z, core, y))]
-
-    for i in range(8):
-        pot_copy(i).wait()
-
-    def gather_step(p, _):
-        off = (p == 0) * 2 + (p == 1) * 1 + (p == 2) * 3
+    def share(t, off):
+        group = (lax.rem(x + off, 4), lax.rem(y + off, 4))
+        return remote(
+            part.at[t, jnp.where(t == 1, group[1], group[0])], r1.at[t, off], rs_sems, 4 * t + off,
+            device(lax.rem(x + (1 - t) * off, 4), z, core, lax.rem(y + t * off, 4)))
+
+    def closing(src, number, to, slot):
+        return pltpu.make_async_remote_copy(
+            src_ref=src, dst_ref=r2.at[slot], send_sem=end_sems.at[0, number],
+            recv_sem=end_sems.at[1, slot], device_id=to, device_id_type=MESH)
+
+    def tiles(t):
+        for zz in range(4):
+            for k in range(4):
+                number = 16 * t + 4 * zz + k
+                if t:
+                    yield s1.at[1, 4 * k + zz], number, device(k, zz, core, y), 4 * z + x, (k == x) & (zz == z)
+                else:
+                    yield s1.at[0, 4 * zz + k], number, device(x, zz + 4, core, k), 4 * z + y, (k == y) & (zz + 4 == z)
+
+    def close(t):
+        for off in range(1, 4):
+            share(t, off).wait_recv()
+        s1[t] = part[t, (x, y)[t]] + r1[t, 1] + r1[t, 2] + r1[t, 3]
+        for src, number, to, slot, mine in tiles(t):
+            @pl.when(jnp.logical_not(mine))
+            def _():
+                closing(src, number, to, slot).start()
+
+            @pl.when(mine)
+            def _():
+                r2[slot] = src[...]
+
+    for i in range(2):
+        pot_copy(lax.rem(lead + i, 8)).wait()
+
+    def gather_step(s, _):
+        t = jnp.where(((s >= 3) & (s < 6)) | (s == 7), 1, 0)
+        third_of = lax.rem(s, 3)
+        off = jnp.where(s >= 6, 0, jnp.where(third_of == 0, 2, jnp.where(third_of == 1, 1, 3)))
         ya, xb = lax.rem(y + off, 4), lax.rem(x + off, 4)
-
-        def part_of_a(xx, _):
+        group = jnp.where(t == 1, ya, xb)
+
+        @pl.when(s == 1)
+        def _():
+            for i in range(2, 8):
+                pot_copy(lax.rem(lead + i, 8)).wait()
+
+        for j in range(4):
+            def number(zz):
+                return jnp.where(t == 1, 4 * j + zz, 4 * zz + j)
+
             def put(zz, v):
-                part_a[ya, xx, zz] = v
-
-            gather_four(xx, 0, ya, lambda zz: 16 * ya + 4 * xx + zz, put)
-            return 0
-
-        def part_of_b(h, _):
-            def put(zz, v):
-                part_b[xb, zz, h] = v
-
-            gather_four(xb, 4, h, lambda zz: 64 + 16 * xb + 4 * zz + h, put)
-            return 0
-
-        lax.fori_loop(0, 4, part_of_b, 0, unroll=True)
-        lax.fori_loop(0, 4, part_of_a, 0, unroll=True)
-        for step, away in enumerate((2, 1, 3)):
-            @pl.when(p == step)
-            def _():
-                launch(shares(away))
+                part[t, group, number(zz)] = v
+
+            gather_four(
+                jnp.where(t == 1, j, xb), 4 - 4 * t, jnp.where(t == 1, ya, j),
+                lambda zz: 64 - 64 * t + 16 * group + number(zz), put)
+
+        @pl.when(s < 6)
+        def _():
+            share(t, off).start()
+
+        @pl.when(s == 6)
+        def _():
+            close(0)
 
         return 0
 
-    lax.fori_loop(0, 4, gather_step, 0)
-    for k in range(1, 4):
-        settle([], shares(k))
-    s1a[...] = part_a[y] + r1[0, 1] + r1[0, 2] + r1[0, 3]
-    s1b[...] = part_b[x] + r1[1, 1] + r1[1, 2] + r1[1, 3]
-
-    def sends(src, lead, to, slot):
-        return pltpu.make_async_remote_copy(
-            src_ref=src, dst_ref=r2.at[slot], send_sem=end_sems.at[0, lead],
-            recv_sem=end_sems.at[1, slot], device_id=to, device_id_type=MESH)
-
-    me_a = 4 * z + x
-    me_b = 4 * z + y
-    outgoing = []
-    for zz in range(4):
-        for k in range(4):
-            outgoing.append((s1a.at[k, zz], device(k, zz, core, y), me_a, (k == x) & (zz == z)))
-            outgoing.append((s1b.at[zz, k], device(x, zz + 4, core, k), me_b, (k == y) & (zz + 4 == z)))
-    for lead, (src, to, slot, mine) in enumerate(outgoing):
-        @pl.when(jnp.logical_not(mine))
-        def _():
-            sends(src, lead, to, slot).start()
-
-        @pl.when(mine)
-        def _():
-            r2[slot] = src[...]
-
-    me = jnp.where(z < 4, me_a, me_b)
+    lax.fori_loop(0, 8, gather_step, 0)
+    close(1)
+    me = jnp.where(z < 4, 4 * z + x, 4 * z + y)
     for slot in range(32):
         @pl.when(slot != me)
         def _():
-            sends(r2.at[slot], 0, sibling, slot).wait_recv()
+            closing(r2.at[slot], 0, sibling, slot).wait_recv()
 
     total = r2[0]
     for slot in range(1, 32):
@@ -593,14 +606,13 @@
     for d in range(3):
         out[d:d + 1, 0:128] = total[2 * d:2 * d + 1, :]
         out[d:d + 1, 128:256] = total[2 * d + 1:2 * d + 2, :]
-    for lead, (src, to, slot, mine) in enumerate(outgoing):
-        @pl.when(jnp.logical_not(mine))
-        def _():
-            sends(src, lead, to, slot).wait_send()
-
-    for k in range(1, 4):
-        for copy in shares(k):
-            copy.wait_send()
+    for t in range(2):
+        for off in range(1, 4):
+            share(t, off).wait_send()
+        for src, number, to, slot, mine in tiles(t):
+            @pl.when(jnp.logical_not(mine))
+            def _():
+                closing(src, number, to, slot).wait_send()
 
 
 def local(charges, grid_base, fraction, counts, influence):
@@ -636,11 +648,9 @@
             f32(N, N),
             f32(64, 2, 8, N),
             f32(64, 2, 8, N),
-            f32(4, 4, 4, *tile),
-            f32(4, 4, 4, *tile),
-            f32(2, 4, 4, 4, *tile),
-            f32(4, 4, *tile),
-            f32(4, 4, *tile),
+            f32(2, 4, 16, *tile),
+            f32(2, 4, 16, *tile),
+            f32(2, 16, *tile),
             f32(32, *tile),
             pltpu.SemaphoreType.DMA((4,)),
             pltpu.SemaphoreType.DMA((2, 32)),

time: 65.9 us -> 65 us (0.986); the launches traced: 65.7 us -> 63.9 us
  Pallas kernels: 63.8 us -> 62 us
    pallas_call x1, Pallas kernels: 63.8 us -> 62 us  [local(): pl.pallas_call(main_kernel, out_shape=jax.ShapeDtypeStruct((3, SLOTS), F3...]
where the time goes in v5:
time: 65 us; the launch traced here: 63.9 us
  Pallas kernels  62 us (95%)
  local copies, waits for them, and re-layouts  1.28 us (2%)
  between operations  0.66 us (1%)
    pallas_call x1, Pallas kernels, local(): pl.pallas_call(main_kernel, out_shape=jax.ShapeDtypeStruct((3, SLOTS), F3...  62 us

profile of v5, /device:TPU:1, one launch (start us, length us, event | category | flops | bytes accessed | tf_op | source)
XLA Modules:
  0.0 63.9 jit_solution(13765967126237322837)
XLA Ops:
  0.7 62.0 %shard_map.91 = f32[3,256]{1,0:T(4,128)} custom-call(s32[1,1]{1,0:T(1,128)S(6)} %copy.11.counts, f32[2,128]{1,0:T(2,128)} %bitcast.3, s32[3,256]{1,0:T(4,128)} %base.1, f32[3,256]{1,0:T(4,128)} %frac.1, f32[2048,128]{1,0:T(8,128)} %bitcast.2, bf16[512,512]{1,0:T(8,128)(2,1)} %constant.8.clone.perm_hbm, bf16[4,2,256,256]{3,2,1,0:T(8,128)(2,1)} %constant.9.clone.mats_hbm, ...), custom_call_target="tpu_custom_call" | custom-call | flops 40000000000 | bytes 4000000 | tf_op jit(solution)/shard_map/pallas_call | solution.py:628
  62.6 1.3 %copy.12 = f32[3,256]{1,0:T(4,128)} copy(f32[3,256]{1,0:T(4,128)} %shard_map.91) | data formatting | bytes 6144

commit v6 on v5

--- a/solution.py
+++ b/solution.py
@@ -229,16 +229,17 @@
            [sender(row_a((x + 4 - k) % 4), row_a((x + 4 - k) % 4), sibling, 8 + k) for k in range(1, 4)]
            + [sender(row_b((y + 4 - k) % 4), row_b((y + 4 - k) % 4), sibling, 12 + k) for k in range(1, 4)])
 
-    def third(k):
-        return [sender(at_a.at[y], at_a.at[y], device(x, z, core, (y + k) % 4), 16 + k),
-                sender(at_b.at[x], at_b.at[x], device((x + k) % 4, z, core, y), 20 + k)]
-
-    def third_from(k):
-        ya, xb = (y + 4 - k) % 4, (x + 4 - k) % 4
-        return [sender(at_a.at[ya], at_a.at[ya], sibling, 16 + k),
-                sender(at_b.at[xb], at_b.at[xb], sibling, 20 + k)]
-
-    launch(third(1) + third(3))
+    def chunk(yy, xx, half, k, to_a, to_b):
+        a, b = at_a.at[yy, pl.ds(8 * half, 8)], at_b.at[xx, pl.ds(2 * half, 2)]
+        return [sender(a, a, to_a, 14 + 2 * k + half), sender(b, b, to_b, 20 + 2 * k + half)]
+
+    def third(k, half):
+        return chunk(y, x, half, k, device(x, z, core, (y + k) % 4), device((x + k) % 4, z, core, y))
+
+    def third_from(k, half):
+        return chunk((y + 4 - k) % 4, (x + 4 - k) % 4, half, k, sibling, sibling)
+
+    launch(third(1, 0) + third(3, 0) + third(1, 1) + third(3, 1))
 
     flat_a = at_a.reshape(64 * 16, 128)
     flat_b = at_b.reshape(64 * 16, 128)
@@ -311,12 +312,9 @@
     def nt(a, b):
         return lax.dot_general(a, b, (((1,), (1,)), ((), ())), preferred_element_type=F32)
 
-    def spread_four(xx, first_z, h, block):
-        here = pl.ds(pl.multiple_of(h * 128, 128), 128)
-        after = pl.ds(pl.multiple_of(lax.rem(h + 1, 4) * 128, 128), 16)
+    def spread_blocks(blocks):
         sums = []
-        for zz in range(4):
-            n = block(zz)
+        for k, h, n in blocks:
             whi, wlo = y_tables(n, WY)
             wtab[0, n] = whi
             wtab[1, n] = wlo
@@ -331,8 +329,9 @@
             dwzd[n] = dw
             both = stack(jnp.concatenate([row(QX + i, n) * w for i in range(4)], axis=0))
             sums.append(halves_sum(nt(both, whi)) + nt(both[:64], wlo))
-        for zz, m in enumerate(sums):
-            k = 8 * xx + first_z + zz
+        for (k, h, n), m in zip(blocks, sums):
+            here = pl.ds(pl.multiple_of(h * 128, 128), 128)
+            after = pl.ds(pl.multiple_of(lax.rem(h + 1, 4) * 128, 128), 16)
             for j, plane in ((0, core), (1, 2)):
                 v = m[32 * j:32 * j + 32]
                 u[plane, k, :, :, here] += v[:, :128].reshape(2, 16, 128)
@@ -341,42 +340,43 @@
     def swap(k):
         return remote(u.at[2, k], u.at[core, k], grid_sems, k, sibling)
 
-    def spread_phase(ya, xb):
-        def part_of_a(xx, _):
-            spread_four(xx, 0, ya, lambda zz: 16 * ya + 4 * xx + zz)
-            return 0
-
-        def part_of_b(h, _):
-            spread_four(xb, 4, h, lambda zz: 64 + 16 * xb + 4 * zz + h)
-            return 0
-
-        def prepare_two(i, _):
-            prepare(flat_a, 2 * ya + i, 0)
-            prepare(flat_b, 2 * xb + i, 64)
-            return 0
-
-        lax.fori_loop(0, 2, prepare_two, 0, unroll=True)
-        lax.fori_loop(0, 4, part_of_b, 0, unroll=True)
-        lax.fori_loop(0, 4, part_of_a, 0, unroll=True)
-        for zz in range(4):
-            swap(8 * xb + 4 + zz).start()
-
     def spread_step(p, _):
         @pl.when(p == 1)
         def _():
-            launch(third(2))
-            settle([], third_from(1))
+            launch(third(2, 0) + third(2, 1))
+            settle([], third_from(1, 0) + third_from(3, 0))
 
         @pl.when(p == 2)
         def _():
-            settle([], third_from(3))
+            settle([], third_from(1, 1) + third_from(3, 1))
 
         @pl.when(p == 3)
         def _():
-            settle([], third_from(2))
-
-        off = lax.rem(3 * p, 4) * (1 - p // 2) + (p // 2) * (p - 1)
-        spread_phase(lax.rem(y + off, 4), lax.rem(x + off, 4))
+            settle([], third_from(2, 0) + third_from(2, 1))
+
+        near = (p == 1) | (p == 2)
+        parts = []
+        for c in range(2):
+            off = jnp.where(near, 3 - 2 * c, jnp.where(p == 3, 2, 0))
+            half = jnp.where(near, p - 1, c)
+            parts.append((lax.rem(y + off, 4), lax.rem(x + off, 4), half))
+        for ya, xb, half in parts:
+            prepare(flat_a, 2 * ya + half, 0)
+            prepare(flat_b, 2 * xb + half, 64)
+        for ya, xb, half in parts:
+            for hp in range(2):
+                spread_blocks([
+                    (8 * xb + 4 + 2 * half + zi, 2 * hp + hi,
+                     64 + 16 * xb + 8 * half + 4 * zi + 2 * hp + hi)
+                    for zi in range(2) for hi in range(2)])
+        for ya, xb, half in parts:
+            for xi in range(2):
+                spread_blocks([
+                    (8 * (2 * half + xi) + zz, ya, 16 * ya + 8 * half + 4 * xi + zz)
+                    for zz in range(4)])
+        for ya, xb, half in parts:
+            for zi in range(2):
+                swap(8 * xb + 4 + 2 * half + zi).start()
         return 0
 
     lax.fori_loop(0, 4, spread_step, 0)
@@ -384,7 +384,7 @@
         for xx in range(4):
             swap(8 * xx + zz).start()
     for k in range(1, 4):
-        for copy in third(k):
+        for copy in third(k, 0) + third(k, 1):
             copy.wait_send()
 
     def grid_landed(k):

time: 65 us -> 62.4 us (0.960); the launches traced: 63.9 us -> 62.1 us
  Pallas kernels: 62 us -> 60.1 us
    pallas_call x1, Pallas kernels: 62 us -> 60.1 us  [local(): pl.pallas_call(main_kernel, out_shape=jax.ShapeDtypeStruct((3, SLOTS), F3...]
where the time goes in v6:
time: 62.4 us; the launch traced here: 62.1 us
  Pallas kernels  60.1 us (96%)
  local copies, waits for them, and re-layouts  1.28 us (2%)
  between operations  0.66 us (1%)
    pallas_call x1, Pallas kernels, local(): pl.pallas_call(main_kernel, out_shape=jax.ShapeDtypeStruct((3, SLOTS), F3...  60.1 us
    unnamed x1, local copies, waits for them, and re-layouts  1.28 us

profile of v6, /device:TPU:1, one launch (start us, length us, event | category | flops | bytes accessed | tf_op | source)
XLA Modules:
  0.0 62.1 jit_solution(17446176288064174128)
XLA Ops:
  0.7 60.1 %shard_map.91 = f32[3,256]{1,0:T(4,128)} custom-call(s32[1,1]{1,0:T(1,128)S(6)} %copy.11.counts, f32[2,128]{1,0:T(2,128)} %bitcast.3, s32[3,256]{1,0:T(4,128)} %base.1, f32[3,256]{1,0:T(4,128)} %frac.1, f32[2048,128]{1,0:T(8,128)} %bitcast.2, bf16[512,512]{1,0:T(8,128)(2,1)} %constant.8.clone.perm_hbm, bf16[4,2,256,256]{3,2,1,0:T(8,128)(2,1)} %constant.9.clone.mats_hbm, ...), custom_call_target="tpu_custom_call" | custom-call | flops 40000000000 | bytes 4000000 | tf_op jit(solution)/shard_map/pallas_call | solution.py:628
  60.8 1.3 %copy.12 = f32[3,256]{1,0:T(4,128)} copy(f32[3,256]{1,0:T(4,128)} %shard_map.91) | data formatting | bytes 6144

commit v7 on v6

--- a/solution.py
+++ b/solution.py
@@ -125,12 +125,12 @@
 
 def peers():
     x, z, c, y = place()
-    yield device(x, z, 1 - c, y)
-    for k in range(1, 4):
+    for k in (4, 3, 5, 2, 6, 1, 7):
+        yield device(x, (z + k) % 8, c, y)
+    for k in (2, 1, 3):
         yield device((x + k) % 4, z, c, y)
         yield device(x, z, c, (y + k) % 4)
-    for k in range(1, 8):
-        yield device(x, (z + k) % 8, c, y)
+    yield device(x, z, 1 - c, y)
 
 
 def greet():
@@ -202,7 +202,7 @@
     met()
 
     first = launch([sender(zbuf.at[z], zbuf.at[z], device(x, (z + k) % 8, core, y), k)
-                    for k in range(1, 8)])
+                    for k in (4, 3, 5, 2, 6, 1, 7)])
     settle(first, [sender(zbuf.at[(z + 8 - k) % 8], zbuf.at[(z + 8 - k) % 8], sibling, k)
                    for k in range(1, 8)])
     for zz in range(4):
@@ -215,9 +215,10 @@
     def row_b(yy):
         return at_b.at[x, :, yy]
 
-    second = launch(
-        [sender(row_a(x), row_a(x), device((x + k) % 4, z, core, y), 8 + k) for k in range(1, 4)]
-        + [sender(row_b(y), row_b(y), device(x, z, core, (y + k) % 4), 12 + k) for k in range(1, 4)])
+    second = launch([
+        copy for k in (2, 1, 3) for copy in (
+            sender(row_a(x), row_a(x), device((x + k) % 4, z, core, y), 8 + k),
+            sender(row_b(y), row_b(y), device(x, z, core, (y + k) % 4), 12 + k))])
     for load in loads:
         load.wait()
     scale = jnp.where(kx == 0, 1.0, 2.0) / float(N) ** 3
@@ -239,7 +240,7 @@
     def third_from(k, half):
         return chunk((y + 4 - k) % 4, (x + 4 - k) % 4, half, k, sibling, sibling)
 
-    launch(third(1, 0) + third(3, 0) + third(1, 1) + third(3, 1))
+    launch(third(1, 0) + third(3, 0) + third(1, 1) + third(3, 1) + third(2, 0) + third(2, 1))
 
     flat_a = at_a.reshape(64 * 16, 128)
     flat_b = at_b.reshape(64 * 16, 128)
@@ -343,7 +344,6 @@
     def spread_step(p, _):
         @pl.when(p == 1)
         def _():
-            launch(third(2, 0) + third(2, 1))
             settle([], third_from(1, 0) + third_from(3, 0))
 
         @pl.when(p == 2)
@@ -536,25 +536,29 @@
 
     def tiles(t):
         for zz in range(4):
+            zt = lax.rem(z + zz, 4)
+            to_z = zt + 4 * (1 - t)
+            ahead = lax.rem(z + 8 - to_z, 8)
             for k in range(4):
-                number = 16 * t + 4 * zz + k
-                if t:
-                    yield s1.at[1, 4 * k + zz], number, device(k, zz, core, y), 4 * z + x, (k == x) & (zz == z)
-                else:
-                    yield s1.at[0, 4 * zz + k], number, device(x, zz + 4, core, k), 4 * z + y, (k == y) & (zz + 4 == z)
+                kt = lax.rem((y, x)[t] + k, 4)
+                src = s1.at[1, 4 * kt + zt] if t else s1.at[0, 4 * zt + kt]
+                to = device(kt, to_z, core, y) if t else device(x, to_z, core, kt)
+                yield zz + k == 0, closing(src, 16 * t + 4 * zz + k, to, 4 * ahead + (4 - k) % 4)
+
+    def each_tile(t, act):
+        for maybe_own, copy in tiles(t):
+            if maybe_own:
+                @pl.when((z >= 4) if t else (z < 4))
+                def _():
+                    act(copy)
+            else:
+                act(copy)
 
     def close(t):
         for off in range(1, 4):
             share(t, off).wait_recv()
         s1[t] = part[t, (x, y)[t]] + r1[t, 1] + r1[t, 2] + r1[t, 3]
-        for src, number, to, slot, mine in tiles(t):
-            @pl.when(jnp.logical_not(mine))
-            def _():
-                closing(src, number, to, slot).start()
-
-            @pl.when(mine)
-            def _():
-                r2[slot] = src[...]
+        each_tile(t, lambda copy: copy.start())
 
     for i in range(2):
         pot_copy(lax.rem(lead + i, 8)).wait()
@@ -594,13 +598,10 @@
 
     lax.fori_loop(0, 8, gather_step, 0)
     close(1)
-    me = jnp.where(z < 4, 4 * z + x, 4 * z + y)
-    for slot in range(32):
-        @pl.when(slot != me)
-        def _():
-            closing(r2.at[slot], 0, sibling, slot).wait_recv()
-
-    total = r2[0]
+    for slot in range(1, 32):
+        closing(r2.at[slot], 0, sibling, slot).wait_recv()
+
+    total = s1[jnp.where(z < 4, 1, 0), jnp.where(z < 4, 4 * x + z, 4 * (z - 4) + y)]
     for slot in range(1, 32):
         total = total + r2[slot]
     for d in range(3):
@@ -609,10 +610,7 @@
     for t in range(2):
         for off in range(1, 4):
             share(t, off).wait_send()
-        for src, number, to, slot, mine in tiles(t):
-            @pl.when(jnp.logical_not(mine))
-            def _():
-                closing(src, number, to, slot).wait_send()
+        each_tile(t, lambda copy: copy.wait_send())
 
 
 def local(charges, grid_base, fraction, counts, influence):

time: 62.4 us -> 61.1 us (0.979)
  Pallas kernels: 60.1 us -> 59 us
    pallas_call x1, Pallas kernels: 60.1 us -> 59 us  [local(): pl.pallas_call(main_kernel, out_shape=jax.ShapeDtypeStruct((3, SLOTS), F3...]
where the time goes in v7:
time: 61.1 us; the launch traced here: 60.9 us
  Pallas kernels  59 us (97%)
  local copies, waits for them, and re-layouts  1.28 us (2%)
  between operations  0.66 us (1%)
    pallas_call x1, Pallas kernels, local(): pl.pallas_call(main_kernel, out_shape=jax.ShapeDtypeStruct((3, SLOTS), F3...  59 us
    unnamed x1, local copies, waits for them, and re-layouts  1.28 us

profile of v7, /device:TPU:1, one launch (start us, length us, event | category | flops | bytes accessed | tf_op | source)
XLA Modules:
  0.0 60.9 jit_solution(2586805075238467906)
XLA Ops:
  0.7 59.0 %shard_map.91 = f32[3,256]{1,0:T(4,128)} custom-call(s32[1,1]{1,0:T(1,128)S(6)} %copy.11.counts, f32[2,128]{1,0:T(2,128)} %bitcast.3, s32[3,256]{1,0:T(4,128)} %base.1, f32[3,256]{1,0:T(4,128)} %frac.1, f32[2048,128]{1,0:T(8,128)} %bitcast.2, bf16[512,512]{1,0:T(8,128)(2,1)} %constant.8.clone.perm_hbm, bf16[4,2,256,256]{3,2,1,0:T(8,128)(2,1)} %constant.9.clone.mats_hbm, ...), custom_call_target="tpu_custom_call" | custom-call | flops 40000000000 | bytes 4000000 | tf_op jit(solution)/shard_map/pallas_call | solution.py:626
  59.6 1.3 %copy.12 = f32[3,256]{1,0:T(4,128)} copy(f32[3,256]{1,0:T(4,128)} %shard_map.91) | data formatting | bytes 6144
